TPU v7x, 32 devices: a whole 2x2x4 slice. The times are simulated.
32 devices in a mesh: dp: 2 (over x), row: 4 (over z), col: 4 (over y, core).
Axes of the slice: x: 2, y: 2, z: 4, core: 2. Of those that a mesh axis runs over, the one named last changes fastest.
Arguments:
- activations: bfloat16 [9232, 1024], P(('dp', 'col'), 'row'), may hold values from -6 to 6
- first_gain: float32 [1024], P('row'), may hold values from 0.5 to 1.5
- first_shift: float32 [1024], P('row'), may hold values from -1.75 to 1.75
- joined_weight: bfloat16 [1024, 3072], P('row', 'col'), may hold values from -0.25 to 0.25
- query_bias: float32 [1024], P('col'), may hold values from -3 to 3
- value_bias: float32 [1024], P('col'), may hold values from -3 to 3
- output_weight: bfloat16 [1024, 1024], P('col', 'row'), may hold values from -0.75 to 0.75
- output_bias: float32 [1024], P('row'), may hold values from -3 to 3
- second_gain: float32 [1024], P('row'), may hold values from 0.5 to 1.5
- second_shift: float32 [1024], P('row'), may hold values from -1.75 to 1.75
- hidden_weight: bfloat16 [1024, 4096], P('row', 'col'), may hold values from -0.1875 to 0.1875
- hidden_bias: float32 [4096], P('col'), may hold values from -3 to 3
- return_weight: bfloat16 [4096, 1024], P('col', 'row'), may hold values from -0.09375 to 0.09375
- return_bias: float32 [1024], P('row'), may hold values from -3 to 3
- layer_grad: bfloat16 [9232, 1024], P(('dp', 'col'), 'row'), may hold values from -6 to 6
Outputs:
- layer_output: bfloat16 [9232, 1024], P(('dp', 'col'), 'row')
- input_grad: float32 [9232, 1024], P(('dp', 'col'), 'row')
- first_gain_grad: float32 [1024], P('row')
- first_shift_grad: float32 [1024], P('row')
- joined_weight_grad: float32 [1024, 3072], P('row', 'col')
- query_bias_grad: float32 [1024], P('col')
- value_bias_grad: float32 [1024], P('col')
- output_weight_grad: float32 [1024, 1024], P('col', 'row')
- output_bias_grad: float32 [1024], P('row')
- second_gain_grad: float32 [1024], P('row')
- second_shift_grad: float32 [1024], P('row')
- hidden_weight_grad: float32 [1024, 4096], P('row', 'col')
- hidden_bias_grad: float32 [4096], P('col')
- return_weight_grad: float32 [4096, 1024], P('col', 'row')
- return_bias_grad: float32 [1024], P('row')
All inputs are finite; a program needn't handle non-finite values.
Results may differ from a plain program's by a relative error of at most 0.012.
The roundings to bfloat16 on the way count: a program that leaves them out, or rounds other values in their place, can miss the bound.
Values may be sent and summed in bfloat16 or wider, within the bound.
A program may use at most 128 MiB of HBM per device.

v0:
```python
import math

import jax
import jax.numpy as jnp
from jax import lax
from jax.sharding import PartitionSpec as P

D = 1024
HEAD_DIM = 64
SEQ = 577


EPSILON = 1e-06
ROOT_HALF = math.sqrt(0.5)
NORMAL_PEAK = 1.0 / math.sqrt(2.0 * math.pi)


def product(left, right):
    return jnp.dot(left, right, preferred_element_type=jnp.float32)


def over_rows(left, right):
    return lax.dot_general(
        left, right, (((0,), (0,)), ((), ())), preferred_element_type=jnp.float32
    )


def against_rows(left, right):
    return lax.dot_general(
        left, right, (((1,), (1,)), ((), ())), preferred_element_type=jnp.float32
    )


def feature_stats(first_terms, second_terms):
    return lax.psum((jnp.sum(first_terms, axis=1), jnp.sum(second_terms, axis=1)), "row")


def gather_tokens(piece_in):
    return lax.all_gather(piece_in, "col", axis=0, tiled=True)


def sum_tokens(piece_in):
    return lax.psum_scatter(piece_in, "col", scatter_dimension=0, tiled=True)


def sum_heads(piece_in):
    return lax.psum_scatter(piece_in, "row", scatter_dimension=1, tiled=True)


def gather_heads(piece_in):
    return lax.all_gather(piece_in, "row", axis=1, tiled=True)


def hidden_sum(piece_in):
    return lax.psum_scatter(piece_in, "row", scatter_dimension=1, tiled=True)


def hidden_spread(piece_in):
    return lax.all_gather(piece_in, "row", axis=1, tiled=True)


def norm_forward(values_in, norm_gain, norm_shift):
    total_sum, square_sum = feature_stats(values_in, values_in * values_in)
    center = total_sum / D
    spread = square_sum / D - center * center
    inv_std = lax.rsqrt(spread + EPSILON)
    normed = (values_in - center[:, None]) * inv_std[:, None]
    return (normed, inv_std, normed * norm_gain + norm_shift)


def norm_backward(grad_in, normed, inv_std, norm_gain):
    scaled = grad_in * norm_gain
    total_sum, along_sum = feature_stats(scaled, scaled * normed)
    return inv_std[:, None] * (scaled - total_sum[:, None] / D - normed * along_sum[:, None] / D)


def gelu_value(inputs):
    return inputs * (lax.erf(inputs * ROOT_HALF) + 1.0) / 2.0


def gelu_slope(inputs):
    return (
        0.5 * (1.0 + lax.erf(inputs * ROOT_HALF))
        + inputs * jnp.exp(-0.5 * inputs * inputs) * NORMAL_PEAK
    )


def attend_forward(image_block):
    query_rows = image_block[:, 0]
    key_rows = image_block[:, 1]
    value_rows = image_block[:, 2]
    scores = against_rows(query_rows, key_rows) * HEAD_DIM ** (-0.5)
    row_max = jnp.max(scores, axis=1, keepdims=True)
    raised = jnp.exp(scores - row_max)
    row_sum = jnp.sum(raised, axis=1, keepdims=True)
    weights_soft = raised / row_sum
    result = product(weights_soft.astype(jnp.bfloat16), value_rows)
    return (result, (row_max + jnp.log(row_sum))[:, 0])


def attend_backward(image_items):
    image_block, grad_rows, log_total = image_items
    query_rows = image_block[:, 0]
    key_rows = image_block[:, 1]
    value_rows = image_block[:, 2]
    attn_scale = HEAD_DIM ** (-0.5)
    scores = against_rows(query_rows, key_rows) * attn_scale
    weights_soft = jnp.exp(scores - log_total[:, None])
    grad_weights = against_rows(grad_rows, value_rows)
    delta_rows = jnp.sum(grad_weights * weights_soft, axis=1, keepdims=True)
    grad_scores = (weights_soft * (grad_weights - delta_rows)).astype(jnp.bfloat16)
    grad_query = product(grad_scores, key_rows) * attn_scale
    grad_key = over_rows(grad_scores, query_rows) * attn_scale
    grad_value = over_rows(weights_soft.astype(jnp.bfloat16), grad_rows)
    return jnp.stack([grad_query, grad_key, grad_value], axis=1)


def body(
    activations,
    first_gain,
    first_shift,
    joined_weight,
    query_bias,
    value_bias,
    output_weight,
    output_bias,
    second_gain,
    second_shift,
    hidden_weight,
    hidden_bias,
    return_weight,
    return_bias,
    layer_grad,
):
    first_row = (lax.axis_index("row") == 0).astype(jnp.float32)
    resid = activations.astype(jnp.float32)
    normed_one, inv_one, first_out = norm_forward(resid, first_gain, first_shift)
    first_full = gather_tokens(first_out.astype(jnp.bfloat16))
    heads_here = query_bias.shape[0] // HEAD_DIM
    zero_part = jnp.zeros((heads_here, HEAD_DIM), jnp.float32)
    joined_bias = jnp.stack(
        [
            query_bias.reshape(heads_here, HEAD_DIM),
            zero_part,
            value_bias.reshape(heads_here, HEAD_DIM),
        ],
        axis=1,
    ).reshape(-1)
    joined_head = sum_heads(product(first_full, joined_weight) + first_row * joined_bias).astype(
        jnp.bfloat16
    )
    blocks = joined_head.reshape(-1, SEQ, 3, HEAD_DIM)
    attended, log_total = lax.map(attend_forward, blocks)
    attended_full = gather_heads(attended.reshape(-1, HEAD_DIM).astype(jnp.bfloat16))
    branch = sum_tokens(product(attended_full, output_weight)) + output_bias
    hidden_in = resid + branch
    normed_two, inv_two, second_out = norm_forward(hidden_in, second_gain, second_shift)
    second_full = gather_tokens(second_out.astype(jnp.bfloat16))
    pre_share = hidden_sum(product(second_full, hidden_weight) + first_row * hidden_bias)
    acted_full = hidden_spread(gelu_value(pre_share).astype(jnp.bfloat16))
    mixed = sum_tokens(product(acted_full, return_weight)) + return_bias
    layer_output = (hidden_in + mixed).astype(jnp.bfloat16)
    grad_out = layer_grad.astype(jnp.float32)
    return_bias_grad = jnp.sum(grad_out, axis=0)
    grad_mixed = gather_tokens(layer_grad)
    return_weight_grad = over_rows(acted_full, grad_mixed)
    grad_acted = hidden_sum(against_rows(grad_mixed, return_weight))
    grad_pre = (grad_acted * gelu_slope(pre_share)).astype(jnp.bfloat16)
    grad_pre_full = hidden_spread(grad_pre)
    hidden_weight_grad = over_rows(second_full, grad_pre_full)
    hidden_bias_grad = jnp.sum(grad_pre_full, axis=0, dtype=jnp.float32)
    grad_second = sum_tokens(against_rows(grad_pre_full, hidden_weight))
    second_gain_grad = jnp.sum(grad_second * normed_two, axis=0)
    second_shift_grad = jnp.sum(grad_second, axis=0)
    grad_hidden = grad_out + norm_backward(grad_second, normed_two, inv_two, second_gain)
    grad_branch = grad_hidden.astype(jnp.bfloat16)
    output_bias_grad = jnp.sum(grad_branch, axis=0, dtype=jnp.float32)
    grad_branch_full = gather_tokens(grad_branch)
    output_weight_grad = over_rows(attended_full, grad_branch_full)
    grad_attended = sum_heads(against_rows(grad_branch_full, output_weight)).astype(jnp.bfloat16)
    grad_blocks = lax.map(
        attend_backward, (blocks, grad_attended.reshape(-1, SEQ, HEAD_DIM), log_total)
    )
    grad_joined = grad_blocks.reshape(-1, 3 * HEAD_DIM).astype(jnp.bfloat16)
    grad_joined_full = gather_heads(grad_joined)
    joined_weight_grad = over_rows(first_full, grad_joined_full)
    bias_terms = jnp.sum(grad_joined_full, axis=0, dtype=jnp.float32).reshape(
        heads_here, 3, HEAD_DIM
    )
    query_bias_grad = bias_terms[:, 0].reshape(-1)
    value_bias_grad = bias_terms[:, 2].reshape(-1)
    grad_first = sum_tokens(against_rows(grad_joined_full, joined_weight))
    first_gain_grad = jnp.sum(grad_first * normed_one, axis=0)
    first_shift_grad = jnp.sum(grad_first, axis=0)
    input_grad = grad_hidden + norm_backward(grad_first, normed_one, inv_one, first_gain)
    (
        first_gain_grad,
        first_shift_grad,
        output_bias_grad,
        second_gain_grad,
        second_shift_grad,
        return_bias_grad,
    ) = lax.psum(
        (
            first_gain_grad,
            first_shift_grad,
            output_bias_grad,
            second_gain_grad,
            second_shift_grad,
            return_bias_grad,
        ),
        ("dp", "col"),
    )
    (
        joined_weight_grad,
        query_bias_grad,
        value_bias_grad,
        output_weight_grad,
        hidden_weight_grad,
        hidden_bias_grad,
        return_weight_grad,
    ) = lax.psum(
        (
            joined_weight_grad,
            query_bias_grad,
            value_bias_grad,
            output_weight_grad,
            hidden_weight_grad,
            hidden_bias_grad,
            return_weight_grad,
        ),
        "dp",
    )
    return (
        layer_output,
        input_grad,
        first_gain_grad,
        first_shift_grad,
        joined_weight_grad,
        query_bias_grad,
        value_bias_grad,
        output_weight_grad,
        output_bias_grad,
        second_gain_grad,
        second_shift_grad,
        hidden_weight_grad,
        hidden_bias_grad,
        return_weight_grad,
        return_bias_grad,
    )


def solution(mesh):
    in_specs = (
        P(("dp", "col"), "row"),
        P("row"),
        P("row"),
        P("row", "col"),
        P("col"),
        P("col"),
        P("col", "row"),
        P("row"),
        P("row"),
        P("row"),
        P("row", "col"),
        P("col"),
        P("col", "row"),
        P("row"),
        P(("dp", "col"), "row"),
    )
    out_specs = (
        P(("dp", "col"), "row"),
        P(("dp", "col"), "row"),
        P("row"),
        P("row"),
        P("row", "col"),
        P("col"),
        P("col"),
        P("col", "row"),
        P("row"),
        P("row"),
        P("row"),
        P("row", "col"),
        P("col"),
        P("col", "row"),
        P("row"),
    )
    return jax.shard_map(body, mesh=mesh, in_specs=in_specs, out_specs=out_specs, check_vma=False)
```

profile of v0, /device:TPU:0, one launch (start us, length us, event | category | flops | bytes accessed | tf_op | source)
XLA Modules:
  0.0 1994.6 jit_solution(4959095097402224977)
XLA Ops:
  7.3 1.5 convert_reduce_fusion.2
  8.8 20.5 %all-reduce.12 = (f32[1154]{0:T(1024)S(1)}, f32[1154]{0:T(1024)S(1)}) all-reduce(f32[1154]{0:T(1024)S(1)} %get-tuple-element.106, f32[1154]{0:T(1024)S(1)} %get-tuple-element.105), channel_id=1, replica_groups=mesh['dp'=2,'row'=4,'col'=4] {'row'}, use_global_device_ids=true, to_apply=%region_3.0 | all-reduce | flops 2308 | bytes 18464 | tf_op jit(solution)/shard_map/psum | solution.py:35
  29.3 2.3 fusion.41
  32.1 22.1 %all-gather.21.cloned.1.call-done = bf16[4,1154,256]{2,1,0:T(8,128)(2,1)} async-done(((bf16[1,1154,256]{2,1,0:T(8,128)(2,1)}), bf16[4,1154,256]{2,1,0:T(8,128)(2,1)}) %all-gather.21.cloned.1.call-update) | async-done | bytes 2363408 | tf_op jit(solution)/shard_map/all_gather | solution.py:39
  54.1 2.3 reshape.98
  56.5 7.3 convolution_add_fusion.1
  63.9 243.6 %reduce-scatter.13.cloned.1.call-done = f32[4616,192]{0,1:T(8,128)} async-done(((f32[4616,768]{0,1:T(8,128)}), f32[4616,192]{0,1:T(8,128)}) %reduce-scatter.13.cloned.1.call-update) | async-done | bytes 3545104 | tf_op jit(solution)/shard_map/reduce_scatter | solution.py:47
  307.5 3.5 convert_element_type.66
  311.0 4.1 reshape.94
  315.1 1.6 copy.38
  316.7 27.7 %while.22 = (s32[]{:T(128)}, bf16[8,577,64]{1,2,0:T(8,128)(2,1)S(1)}, f32[8,577]{1,0:T(8,128)}, bf16[8,577,3,64]{1,3,2,0:T(8,128)(2,1)}, s32[]{:T(128)}, /*index=5*/s32[]{:T(128)}) while((s32[]{:T(128)}, bf16[8,577,64]{1,2,0:T(8,128)(2,1)S(1)}, f32[8,577]{1,0:T(8,128)}, bf16[8,577,3,64]{1,3,2,0:T(8,128)(2,1)}, s32[]{:T(128)}, ...), condition=%wide.region_8.9_spmd, body=%wide.region_5.8_spmd.sunk | while | flops 87559744 | bytes 5042561 | solution.py:153
  346.7 52.1 %all-gather.13.cloned.1.call-done = bf16[4616,256]{0,1:T(8,128)(2,1)} async-done(((bf16[4616,64]{0,1:T(8,128)(2,1)}), bf16[4616,256]{0,1:T(8,128)(2,1)}) %all-gather.13.cloned.1.call-update) | async-done | bytes 2363408 | tf_op jit(solution)/shard_map/all_gather | solution.py:51
  398.9 4.6 fusion.45
  403.5 56.8 %fusion = f32[1160,256]{1,0:T(8,128)S(1)} fusion(f32[4616,256]{1,0:T(8,128)} %fusion.45), kind=kCustom, calls=%all-reduce-scatter | all-reduce-scatter fusion | flops 1187841 | bytes 5915136
  460.3 1.4 collective-permute-start
  463.0 3.6 concatenate
  466.7 1.8 fusion.42
  468.5 18.2 all-reduce.11
  488.2 3.7 reshape.102
  491.9 9.6 fusion.47
  502.2 9.8 all-gather.23.cloned.1.call-done
  512.0 2.3 reshape.100
  514.3 8.4 convolution_add_fusion
  522.8 305.9 %reduce-scatter.17.cloned.1.call-done = f32[4616,256]{1,0:T(8,128)} async-done(((f32[4616,1024]{1,0:T(8,128)}), f32[4616,256]{1,0:T(8,128)}) %reduce-scatter.17.cloned.1.call-update) | async-done | bytes 4726800 | tf_op jit(solution)/shard_map/reduce_scatter | solution.py:55
  828.7 317.9 %reduce-scatter.15.cloned.1.call-done = f32[4616,256]{1,0:T(8,128)} async-done(((f32[4616,1024]{1,0:T(8,128)}), f32[4616,256]{1,0:T(8,128)}) %reduce-scatter.15.cloned.1.call-update) | async-done | bytes 4726800 | tf_op jit(solution)/shard_map/reduce_scatter | solution.py:55
  1146.5 6.6 fusion.23
  1153.2 167.7 %all-gather.17.cloned.1.call-done = bf16[4616,1024]{1,0:T(8,128)(2,1)} async-done(((bf16[4616,256]{1,0:T(8,128)(2,1)}), bf16[4616,1024]{1,0:T(8,128)(2,1)}) %all-gather.17.cloned.1.call-update) | async-done | bytes 9453584 | tf_op jit(solution)/shard_map/all_gather | solution.py:59
  1320.9 8.6 fusion.48
  1329.5 46.3 %fusion.2 = f32[1160,256]{1,0:T(8,128)} fusion(f32[4616,256]{1,0:T(8,128)} %fusion.48), kind=kCustom, calls=%all-reduce-scatter.2 | all-reduce-scatter fusion | flops 1187841 | bytes 5915136
  1378.6 4.6 concatenate.2
  1383.2 3.0 multiply_reduce_fusion.1
  1386.2 15.9 all-reduce.10
  1402.1 2.8 convert_reduce_fusion.4
  1407.4 24.1 %all-gather.27.cloned.1.call-done = bf16[4,1154,256]{2,1,0:T(8,128)(2,1)} async-done(((bf16[1,1154,256]{2,1,0:T(8,128)(2,1)}), bf16[4,1154,256]{2,1,0:T(8,128)(2,1)}) %all-gather.27.cloned.1.call-update) | async-done | bytes 2363408 | tf_op jit(solution)/shard_map/all_gather | solution.py:39
  1431.5 3.7 reshape.104
  1435.1 4.7 fusion.49
  1440.7 86.8 %reduce-scatter.19.cloned.1.call-done = f32[4616,64]{0,1:T(8,128)} async-done(((f32[4616,256]{0,1:T(8,128)}), f32[4616,64]{0,1:T(8,128)}) %reduce-scatter.19.cloned.1.call-update) | async-done | bytes 1181712 | tf_op jit(solution)/shard_map/reduce_scatter | solution.py:47
  1527.4 2.2 convert_element_type.75
  1529.6 2.7 reshape.95
  1532.3 2.4 copy.41
  1534.7 51.1 %while.23 = (s32[]{:T(128)}, bf16[8,577,3,64]{1,3,2,0:T(8,128)(2,1)}, bf16[8,577,3,64]{1,3,2,0:T(8,128)(2,1)}, f32[8,577]{1,0:T(8,128)}, bf16[8,577,64]{2,1,0:T(8,128)(2,1)}, /*index=5*/s32[]{:T(128)}) while((s32[]{:T(128)}, bf16[8,577,3,64]{1,3,2,0:T(8,128)(2,1)}, bf16[8,577,3,64]{1,3,2,0:T(8,128)(2,1)}, f32[8,577]{1,0:T(8,128)}, ...), condition=%wide.region_25.26_spmd, body=%wide.region_23.25_spmd.sunk | while | flops 216549824 | bytes 12170099 | solution.py:181
  1536.9 1.4 multiply_reduce_fusion.7
  1585.8 3.9 copy.42
  1589.7 4.3 convert_element_type.77
  1594.1 5.1 convert_reduce_fusion
  1599.3 96.9 %all-gather.15.cloned.1.call-done = bf16[4616,1024]{1,0:T(8,128)(2,1)} async-done(((bf16[4616,256]{1,0:T(8,128)(2,1)}), bf16[4616,1024]{1,0:T(8,128)(2,1)}) %all-gather.15.cloned.1.call-update) | async-done | bytes 9453584 | tf_op jit(solution)/shard_map/all_gather | solution.py:59
  1696.2 9.1 fusion.46
  1705.3 8.2 fusion.53
  1713.6 4.3 fusion.54
  1717.9 1.5 fusion.52
  1719.4 107.9 %all-gather.19.cloned.1.call-done = bf16[4616,768]{0,1:T(8,128)(2,1)} async-done(((bf16[4616,192]{0,1:T(8,128)(2,1)}), bf16[4616,768]{0,1:T(8,128)(2,1)}) %all-gather.19.cloned.1.call-update) | async-done | bytes 7090192 | tf_op jit(solution)/shard_map/all_gather | solution.py:51
  1827.3 6.8 fusion.51
  1835.1 7.5 fusion.50
  1842.6 83.7 %fusion.43 = (f32[1160,256]{1,0:T(8,128)S(1)}, f32[1160,256]{1,0:T(8,128)S(1)}) fusion(f32[4616,256]{1,0:T(8,128)} %fusion.46, f32[4616,256]{1,0:T(8,128)} %fusion.50), kind=kCustom, calls=%all-reduce-scatter.4 | all-reduce-scatter fusion | flops 2375681 | bytes 11829760
  1926.4 4.5 convert_reduce_fusion.1
  1932.3 3.9 collective-permute-start.1
  1936.4 5.6 all-reduce.13
  1941.9 3.2 concatenate.3
  1945.2 3.6 concatenate.1
  1949.8 12.6 all-reduce.8
  1962.4 16.4 all-reduce.9
  1978.8 2.4 fusion.39
  1981.2 1.8 fusion.35
  1983.0 2.2 copy.67
  (272 shorter events, 94.9 us)
Async XLA Ops:
  7.2 507.1 %copy-start = (bf16[256,1024]{1,0:T(8,128)(2,1)S(1)}, bf16[256,1024]{1,0:T(8,128)(2,1)}, u32[]{:S(2)}) copy-start(bf16[256,1024]{1,0:T(8,128)(2,1)} %param.29) | copy-start | bytes 1572868
  7.2 24.5 %copy-start.34 = (f32[256]{0:T(256)S(1)}, f32[256]{0:T(256)}, u32[]{:S(2)}) copy-start(f32[256]{0:T(256)} %param.23) | copy-start | bytes 3076
  7.2 24.6 %copy-start.35 = (f32[256]{0:T(256)S(1)}, f32[256]{0:T(256)}, u32[]{:S(2)}) copy-start(f32[256]{0:T(256)} %param.24) | copy-start | bytes 3076
  7.2 46.9 %all-gather.21.cloned.1.call-start = ((), (), s32[]{:S(2)}) async-start(), calls=%async_computation.12 | async-start | bytes 2969600 | tf_op jit(solution)/shard_map/all_gather | solution.py:39
  29.3 2.8 copy-start.23
  31.6 275.9 %reduce-scatter.13.cloned.1.call-start = ((), (), s32[]{:S(2)}) async-start(), calls=%async_computation.4 | async-start | bytes 18186240 | tf_op jit(solution)/shard_map/reduce_scatter | solution.py:47
  32.1 24.4 %copy-start.14 = (bf16[256,768]{1,0:T(8,128)(2,1)S(1)}, bf16[256,768]{1,0:T(8,128)(2,1)}, u32[]{:S(2)}) copy-start(bf16[256,768]{1,0:T(8,128)(2,1)} %param.22) | copy-start | bytes 1179652
  56.4 7.3 copy-start.7
  63.8 335.1 %all-gather.13.cloned.1.call-start = ((), (), s32[]{:S(2)}) async-start(), calls=%async_computation.5 | async-start | bytes 3031040 | tf_op jit(solution)/shard_map/all_gather | solution.py:51
  344.7 54.2 %copy-start.20 = (bf16[256,256]{1,0:T(8,128)(2,1)S(1)}, bf16[256,256]{1,0:T(8,128)(2,1)}, u32[]{:S(2)}) copy-start(bf16[256,256]{1,0:T(8,128)(2,1)} %param.25) | copy-start | bytes 393220
  346.1 142.1 %all-gather.25.cloned.1.call-start = ((), (), s32[]{:S(2)}) async-start(), calls=%async_computation.14 | async-start | bytes 2969600 | tf_op jit(solution)/shard_map/all_gather | solution.py:39
  346.7 165.3 %all-gather.23.cloned.1.call-start = ((), (), s32[]{:S(2)}) async-start(), calls=%async_computation.13 | async-start | bytes 2969600 | tf_op jit(solution)/shard_map/all_gather | solution.py:39
  403.5 58.3 %copy-start.36 = (u32[32]{0:T(128)S(1)}, u32[32]{0:T(128)}, u32[]{:S(2)}) copy-start(u32[32]{0:T(128)} %constant.77) | copy-start | bytes 388
  460.3 6.3 copy-start.5
  460.3 6.3 copy-start.31
  460.3 2.7 collective-permute-start
  466.6 20.0 %copy-start.25 = (f32[256]{0:T(256)S(1)}, f32[256]{0:T(256)}, u32[]{:S(2)}) copy-start(f32[256]{0:T(256)} %param.27) | copy-start | bytes 3076
  466.7 20.0 %copy-start.32 = (f32[256]{0:T(256)S(1)}, f32[256]{0:T(256)}, u32[]{:S(2)}) copy-start(f32[256]{0:T(256)} %param.28) | copy-start | bytes 3076
  468.5 23.5 %copy-start.2 = (f32[1154,256]{1,0:T(8,128)}, f32[1154,256]{1,0:T(8,128)S(1)}, u32[]{:S(2)}) copy-start(f32[1154,256]{1,0:T(8,128)S(1)} %get-tuple-element.154) | copy-start | bytes 3545092
  487.9 4.0 copy-start.18
  487.9 340.8 %reduce-scatter.17.cloned.1.call-start = ((), (), s32[]{:S(2)}) async-start(), calls=%async_computation.8 | async-start | bytes 23633920 | tf_op jit(solution)/shard_map/reduce_scatter | solution.py:55
  501.5 0.7 copy-start.30
  501.5 645.0 %reduce-scatter.15.cloned.1.call-start = ((), (), s32[]{:S(2)}) async-start(), calls=%async_computation.6 | async-start | bytes 23633920 | tf_op jit(solution)/shard_map/reduce_scatter | solution.py:55
  522.7 798.1 %all-gather.17.cloned.1.call-start = ((), (), s32[]{:S(2)}) async-start(), calls=%async_computation.9 | async-start | bytes 11816960 | tf_op jit(solution)/shard_map/all_gather | solution.py:59
  1153.1 278.3 %all-gather.27.cloned.1.call-start = ((), (), s32[]{:S(2)}) async-start(), calls=%async_computation.15 | async-start | bytes 2969600 | tf_op jit(solution)/shard_map/all_gather | solution.py:39
  1376.5 2.1 collective-permute-start.2
  1405.0 1.0 copy-start.8
  1406.9 28.2 %copy-start.21 = (bf16[256,256]{1,0:T(8,128)(2,1)S(1)}, bf16[256,256]{1,0:T(8,128)(2,1)}, u32[]{:S(2)}) copy-start(bf16[256,256]{1,0:T(8,128)(2,1)} %param.25) | copy-start | bytes 393220
  1406.9 120.5 %reduce-scatter.19.cloned.1.call-start = ((), (), s32[]{:S(2)}) async-start(), calls=%async_computation.10 | async-start | bytes 6062080 | tf_op jit(solution)/shard_map/reduce_scatter | solution.py:47
  1439.9 256.3 %all-gather.15.cloned.1.call-start = ((), (), s32[]{:S(2)}) async-start(), calls=%async_computation.7 | async-start | bytes 11816960 | tf_op jit(solution)/shard_map/all_gather | solution.py:59
  1440.6 386.7 %all-gather.19.cloned.1.call-start = ((), (), s32[]{:S(2)}) async-start(), calls=%async_computation.11 | async-start | bytes 9093120 | tf_op jit(solution)/shard_map/all_gather | solution.py:51
  1594.0 102.1 %copy-start.19 = (bf16[1024,256]{1,0:T(8,128)(2,1)S(1)}, bf16[1024,256]{1,0:T(8,128)(2,1)}, u32[]{:S(2)}) copy-start(bf16[1024,256]{1,0:T(8,128)(2,1)} %param.31) | copy-start | bytes 1572868
  1594.1 388.9 %all-reduce.18.cloned.1.call-start = ((), (), s32[]{:S(2)}) async-start(), calls=%async_computation.16 | async-start | bytes 6291456 | tf_op jit(solution)/shard_map/psum | solution.py:222
  1696.2 17.3 slice-start
  1696.2 17.3 slice-start.1
  1705.3 8.3 copy-start.4
  1705.3 8.3 slice-start.2
  1713.5 4.3 copy-start.6
  1713.6 4.3 copy-start.13
  1834.1 1.0 copy-start.15
  1926.4 4.6 copy-start.12
  1931.0 10.9 collective-permute-start.3
  1932.3 12.9 collective-permute-start.1
  1945.1 4.6 copy-start.10
  1945.2 3.7 copy-start.24
  1945.2 3.7 copy-start.26
  1948.8 0.9 copy-start.27
  1948.8 0.9 copy-start.28
  1948.8 0.9 copy-start.29
  1948.9 29.9 %copy-start.3 = (f32[1154,256]{1,0:T(8,128)S(1)}, f32[1154,256]{1,0:T(8,128)}, u32[]{:S(2)}) copy-start(f32[1154,256]{1,0:T(8,128)} %copy-done.2) | copy-start | bytes 3545092
  1948.9 29.9 %copy-start.33 = (f32[256]{0:T(256)S(1)}, f32[256]{0:T(256)}, u32[]{:S(2)}) copy-start(f32[256]{0:T(256)} %param.32) | copy-start | bytes 3076
  1978.7 2.5 copy-start.9
  1978.7 2.5 copy-start.11
  1983.0 2.2 copy-start.22
  1983.0 2.9 copy-start.17
  1985.1 1.7 copy-start.16
  1985.9 1.9 copy-start.1
Sparse Core Ops, SparseCore 0:
  31.7 22.3 all-gather.20
  63.9 243.5 reduce-scatter.12
  346.2 52.6 all-gather.12
  400.4 34.2 all-gather.24
  488.0 23.9 all-gather.22
  514.4 314.2 reduce-scatter.16
  831.2 315.3 reduce-scatter.14
  1153.3 167.5 all-gather.16
  1407.0 24.3 all-gather.26
  1440.0 87.3 reduce-scatter.18
  1529.1 167.0 all-gather.14
  1697.7 129.5 all-gather.18
  1834.3 84.5 all-reduce.17
where the time goes:
time: 2010 us; the launch traced here: 1990 us
  waiting for transfers between devices  1440 us (72%)
  blocking collectives  276 us (14%)
  matrix products  117 us (6%)
  local copies, waits for them, and re-layouts  89.7 us (4%)
  other arithmetic  50.1 us (2%)
    reduce_scatter x2, waiting for transfers between devices, hidden_sum(): return lax.psum_scatter(piece_in, 'row', scatter_dimension=1, tiled=True)  624 us
    reduce_scatter x2, waiting for transfers between devices, sum_heads(): return lax.psum_scatter(piece_in, 'row', scatter_dimension=1, tiled=True)  330 us
    all_gather x2, waiting for transfers between devices, hidden_spread(): return lax.all_gather(piece_in, 'row', axis=1, tiled=True)  265 us
    unnamed x3, blocking collectives  187 us
    all_gather x2, waiting for transfers between devices, gather_heads(): return lax.all_gather(piece_in, 'row', axis=1, tiled=True)  160 us
    psum x4, blocking collectives, feature_stats(): lax.psum((jnp.sum(first_terms, axis=1), jnp.sum(second_terms, axis=1)), '...  70.9 us
    all_gather x4, waiting for transfers between devices, gather_tokens(): return lax.all_gather(piece_in, 'col', axis=0, tiled=True)  56 us
    dot_general x28, matrix products, against_rows(): lax.dot_general(left, right, (((1,), (1,)), ((), ())), preferred_element_...  48.5 us
  transfers between devices with their start and end apart: 17, of which 12 were waited for; matrix products, arithmetic and copies ran while one was open for 15% of the time, Pallas kernels for 0%

commit v1 on v0

v1 whole, which is shorter than its diff:
```python
import math

import jax
import jax.numpy as jnp
from jax import lax
from jax.sharding import Mesh
from jax.sharding import PartitionSpec as P

D = 1024
HEAD_DIM = 64
SEQ = 577


EPSILON = 1e-06
ROOT_HALF = math.sqrt(0.5)
NORMAL_PEAK = 1.0 / math.sqrt(2.0 * math.pi)


def product(left, right):
    return jnp.dot(left, right, preferred_element_type=jnp.float32)


def over_rows(left, right):
    return lax.dot_general(
        left, right, (((0,), (0,)), ((), ())), preferred_element_type=jnp.float32
    )


def against_rows(left, right):
    return lax.dot_general(
        left, right, (((1,), (1,)), ((), ())), preferred_element_type=jnp.float32
    )


def swap_cores(piece):
    return lax.ppermute(piece, "core", [(0, 1), (1, 0)])


def core_sum(piece):
    return piece + swap_cores(piece)


def by_core(mine, other, axis):
    first = lax.axis_index("core") == 0
    return jnp.stack([jnp.where(first, mine, other), jnp.where(first, other, mine)], axis=axis)


def images_in(pieces):
    k = lax.axis_index("core")
    count, local, width = pieces.shape
    halves = pieces.reshape(count, local // SEQ, SEQ, 2, width // 2)
    mine = lax.dynamic_index_in_dim(halves, k, 3, keepdims=False)
    other = swap_cores(lax.dynamic_index_in_dim(halves, 1 - k, 3, keepdims=False))
    column = by_core(mine, other, 1).reshape(count, 2 * local // SEQ, SEQ, width // 2)
    chip = lax.all_to_all(column, "row", split_axis=1, concat_axis=3, tiled=True)
    rows = lax.axis_size("row")
    chip = chip.reshape(count, -1, rows, width // 2)
    return by_core(chip, swap_cores(chip), 3).reshape(count, -1, rows * width)


def images_out(values):
    k = lax.axis_index("core")
    rows = lax.axis_size("row")
    tokens, total = values.shape
    half = total // rows // 2
    mine = lax.dynamic_index_in_dim(values.reshape(tokens, rows, 2, half), k, 2, keepdims=False)
    mine = mine.reshape(tokens // SEQ, SEQ, rows * half)
    column = lax.all_to_all(mine, "row", split_axis=2, concat_axis=0, tiled=True)
    column = column.reshape(2, -1, half)
    kept = lax.dynamic_index_in_dim(column, k, 0, keepdims=False)
    other = swap_cores(lax.dynamic_index_in_dim(column, 1 - k, 0, keepdims=False))
    return by_core(kept, other, 1).reshape(-1, 2 * half)


def gather_blocks(block, split_columns):
    rows, pair = lax.axis_size("row"), lax.axis_size("y")
    high, wide = block.shape
    found = lax.all_gather(block, ("row", "y")).reshape(rows, pair, high, wide)
    if split_columns:
        return jnp.transpose(found, (1, 2, 0, 3)).reshape(pair * high, rows * wide)
    return jnp.transpose(found, (0, 2, 1, 3)).reshape(rows * high, pair * wide)


def scatter_blocks(grad, split_columns):
    rows, pair = lax.axis_size("row"), lax.axis_size("y")
    grad = grad.astype(jnp.bfloat16)
    high, wide = grad.shape
    if split_columns:
        parts = jnp.transpose(grad.reshape(pair, high // pair, rows, wide // rows), (2, 0, 1, 3))
    else:
        parts = jnp.transpose(grad.reshape(rows, high // rows, pair, wide // pair), (0, 2, 1, 3))
    parts = parts.reshape(rows * pair, *parts.shape[2:])
    share = lax.psum_scatter(parts, ("row", "y"), scatter_dimension=0)
    if lax.axis_size("dp") == 2:
        other = lax.ppermute(share, "dp", [(0, 1), (1, 0)])
        return share.astype(jnp.float32) + other.astype(jnp.float32)
    return lax.psum(share, "dp").astype(jnp.float32)


def norm_forward(values_in, norm_gain, norm_shift):
    center = jnp.mean(values_in, axis=1, keepdims=True)
    spread = jnp.mean(values_in * values_in, axis=1, keepdims=True) - center * center
    inv_std = lax.rsqrt(spread + EPSILON)
    normed = (values_in - center) * inv_std
    return (normed, inv_std, normed * norm_gain + norm_shift)


def norm_backward(grad_in, normed, inv_std, norm_gain):
    scaled = grad_in * norm_gain
    total = jnp.mean(scaled, axis=1, keepdims=True)
    along = jnp.mean(scaled * normed, axis=1, keepdims=True)
    return inv_std * (scaled - total - normed * along)


def gelu_value(inputs):
    return inputs * (lax.erf(inputs * ROOT_HALF) + 1.0) / 2.0


def gelu_slope(inputs):
    return (
        0.5 * (1.0 + lax.erf(inputs * ROOT_HALF))
        + inputs * jnp.exp(-0.5 * inputs * inputs) * NORMAL_PEAK
    )


def attend_forward(image_block):
    query_rows = image_block[0]
    key_rows = image_block[1]
    value_rows = image_block[2]
    scores = against_rows(query_rows, key_rows) * HEAD_DIM ** (-0.5)
    row_max = jnp.max(scores, axis=1, keepdims=True)
    raised = jnp.exp(scores - row_max)
    row_sum = jnp.sum(raised, axis=1, keepdims=True)
    weights_soft = raised / row_sum
    result = product(weights_soft.astype(jnp.bfloat16), value_rows)
    return (result, (row_max + jnp.log(row_sum))[:, 0])


def attend_backward(image_items):
    image_block, grad_rows, log_total = image_items
    query_rows = image_block[0]
    key_rows = image_block[1]
    value_rows = image_block[2]
    attn_scale = HEAD_DIM ** (-0.5)
    scores = against_rows(query_rows, key_rows) * attn_scale
    weights_soft = jnp.exp(scores - log_total[:, None])
    grad_weights = against_rows(grad_rows, value_rows)
    delta_rows = jnp.sum(grad_weights * weights_soft, axis=1, keepdims=True)
    grad_scores = (weights_soft * (grad_weights - delta_rows)).astype(jnp.bfloat16)
    grad_query = product(grad_scores, key_rows) * attn_scale
    grad_key = over_rows(grad_scores, query_rows) * attn_scale
    grad_value = over_rows(weights_soft.astype(jnp.bfloat16), grad_rows)
    return jnp.stack([grad_query, grad_key, grad_value], axis=0)


def body(
    activations,
    first_gain,
    first_shift,
    joined_weight,
    query_bias,
    value_bias,
    output_weight,
    output_bias,
    second_gain,
    second_shift,
    hidden_weight,
    hidden_bias,
    return_weight,
    return_bias,
    layer_grad,
):
    k = lax.axis_index("core")
    rows = lax.axis_size("row")
    pair = lax.axis_size("y")
    width = activations.shape[1]
    chip_images = 2 * activations.shape[0] // SEQ // rows
    tokens = chip_images * SEQ
    block_heads = query_bias.shape[0] // HEAD_DIM
    heads = pair * block_heads

    joined_all = gather_blocks(joined_weight, False)
    small_all = lax.all_gather(
        jnp.concatenate(
            [
                first_gain,
                first_shift,
                output_bias,
                second_gain,
                second_shift,
                return_bias,
                query_bias,
                value_bias,
                hidden_bias,
            ]
        ),
        ("row", "y"),
    ).reshape(rows, pair, -1)
    wide = small_all[:, 0, : 6 * width].reshape(rows, 6, width)
    wide = jnp.transpose(wide, (1, 0, 2)).reshape(6, -1)
    gain_one, shift_one, out_bias, gain_two, shift_two, ret_bias = (wide[i] for i in range(6))
    deep = small_all[0, :, 6 * width :]
    cut = query_bias.shape[0]
    q_bias = deep[:, :cut].reshape(heads, HEAD_DIM)
    v_bias = deep[:, cut : 2 * cut].reshape(heads, HEAD_DIM)
    h_bias = deep[:, 2 * cut :].reshape(-1)
    joined_bias = jnp.stack([q_bias, jnp.zeros_like(q_bias), v_bias], axis=1).reshape(-1)

    resid, layer_g = images_in(jnp.stack([activations, layer_grad]))
    output_all = gather_blocks(output_weight, True)
    hidden_all = gather_blocks(hidden_weight, False)
    return_all = gather_blocks(return_weight, True)
    resid = resid.astype(jnp.float32)
    normed_one, inv_one, first_out = norm_forward(resid, gain_one, shift_one)
    first_out = first_out.astype(jnp.bfloat16)
    joined = (product(first_out, joined_all) + joined_bias).astype(jnp.bfloat16)
    blocks = jnp.transpose(
        joined.reshape(chip_images, SEQ, heads, 3, HEAD_DIM), (0, 2, 3, 1, 4)
    ).reshape(-1, 3, SEQ, HEAD_DIM)
    attended, log_total = lax.map(attend_forward, blocks)
    attended = jnp.transpose(
        attended.astype(jnp.bfloat16).reshape(chip_images, heads, SEQ, HEAD_DIM), (0, 2, 1, 3)
    ).reshape(tokens, -1)
    branch = core_sum(product(attended, output_all)) + out_bias
    hidden_in = resid + branch
    normed_two, inv_two, second_out = norm_forward(hidden_in, gain_two, shift_two)
    second_out = second_out.astype(jnp.bfloat16)
    pre_act = product(second_out, hidden_all) + h_bias
    acted = gelu_value(pre_act).astype(jnp.bfloat16)
    mixed = core_sum(product(acted, return_all)) + ret_bias
    layer_output = images_out((hidden_in + mixed).astype(jnp.bfloat16))

    grad_out = layer_g.astype(jnp.float32)
    return_weight_grad = scatter_blocks(over_rows(acted, layer_g), True)
    grad_acted = against_rows(layer_g, return_all)
    grad_pre = (grad_acted * gelu_slope(pre_act)).astype(jnp.bfloat16)
    hidden_weight_grad = scatter_blocks(over_rows(second_out, grad_pre), False)
    grad_second = core_sum(against_rows(grad_pre, hidden_all))
    grad_hidden = grad_out + norm_backward(grad_second, normed_two, inv_two, gain_two)
    grad_branch = grad_hidden.astype(jnp.bfloat16)
    output_weight_grad = scatter_blocks(over_rows(attended, grad_branch), True)
    grad_attended = against_rows(grad_branch, output_all).astype(jnp.bfloat16)
    grad_heads = jnp.transpose(
        grad_attended.reshape(chip_images, SEQ, heads, HEAD_DIM), (0, 2, 1, 3)
    ).reshape(-1, SEQ, HEAD_DIM)
    grad_blocks = lax.map(attend_backward, (blocks, grad_heads, log_total))
    grad_joined = jnp.transpose(
        grad_blocks.astype(jnp.bfloat16).reshape(chip_images, heads, 3, SEQ, HEAD_DIM),
        (0, 3, 1, 2, 4),
    ).reshape(tokens, -1)
    joined_weight_grad = scatter_blocks(over_rows(first_out, grad_joined), False)
    grad_first = core_sum(against_rows(grad_joined, joined_all))
    input_grad = images_out(
        (grad_hidden + norm_backward(grad_first, normed_one, inv_one, gain_one)).astype(
            jnp.bfloat16
        )
    ).astype(jnp.float32)

    joined_terms = jnp.sum(grad_joined, axis=0, dtype=jnp.float32).reshape(
        pair, block_heads, 3, HEAD_DIM
    )
    wide_sums = jnp.stack(
        [
            jnp.sum(grad_first * normed_one, axis=0),
            jnp.sum(grad_first, axis=0),
            jnp.sum(grad_branch, axis=0, dtype=jnp.float32),
            jnp.sum(grad_second * normed_two, axis=0),
            jnp.sum(grad_second, axis=0),
            jnp.sum(grad_out, axis=0),
        ]
    )
    deep_sums = jnp.concatenate(
        [
            joined_terms[:, :, 0].reshape(pair, -1),
            joined_terms[:, :, 2].reshape(pair, -1),
            jnp.sum(grad_pre, axis=0, dtype=jnp.float32).reshape(pair, -1),
        ],
        axis=1,
    )
    sums = lax.psum(
        jnp.concatenate([wide_sums.reshape(-1), deep_sums.reshape(-1)]), ("dp", "row", "y")
    )
    wide_sums = sums[: wide_sums.size].reshape(6, rows, width)
    deep_sums = sums[wide_sums.size :].reshape(pair, -1)
    wide_sums = lax.dynamic_index_in_dim(wide_sums, lax.axis_index("row"), 1, keepdims=False)
    deep_sums = lax.dynamic_index_in_dim(deep_sums, lax.axis_index("y"), 0, keepdims=False)
    (
        first_gain_grad,
        first_shift_grad,
        output_bias_grad,
        second_gain_grad,
        second_shift_grad,
        return_bias_grad,
    ) = (wide_sums[i] for i in range(6))
    query_bias_grad = deep_sums[:cut]
    value_bias_grad = deep_sums[cut : 2 * cut]
    hidden_bias_grad = deep_sums[2 * cut :]
    return (
        layer_output,
        input_grad,
        first_gain_grad,
        first_shift_grad,
        joined_weight_grad,
        query_bias_grad,
        value_bias_grad,
        output_weight_grad,
        output_bias_grad,
        second_gain_grad,
        second_shift_grad,
        hidden_weight_grad,
        hidden_bias_grad,
        return_weight_grad,
        return_bias_grad,
    )


def solution(mesh):
    shape = mesh.shape
    mesh = Mesh(
        mesh.devices.reshape(shape["dp"], shape["row"], shape["col"] // 2, 2),
        ("dp", "row", "y", "core"),
    )
    in_specs = (
        P(("dp", "y", "core"), "row"),
        P("row"),
        P("row"),
        P("row", ("y", "core")),
        P(("y", "core")),
        P(("y", "core")),
        P(("y", "core"), "row"),
        P("row"),
        P("row"),
        P("row"),
        P("row", ("y", "core")),
        P(("y", "core")),
        P(("y", "core"), "row"),
        P("row"),
        P(("dp", "y", "core"), "row"),
    )
    out_specs = (
        P(("dp", "y", "core"), "row"),
        P(("dp", "y", "core"), "row"),
        P("row"),
        P("row"),
        P("row", ("y", "core")),
        P(("y", "core")),
        P(("y", "core")),
        P(("y", "core"), "row"),
        P("row"),
        P("row"),
        P("row"),
        P("row", ("y", "core")),
        P(("y", "core")),
        P(("y", "core"), "row"),
        P("row"),
    )
    return jax.shard_map(body, mesh=mesh, in_specs=in_specs, out_specs=out_specs, check_vma=False)
```

time: 2010 us -> 686 us (0.34)
  waiting for transfers between devices: 1440 us -> 183 us
  blocking collectives: 276 us -> 135 us
  local copies, waits for them, and re-layouts: 89.7 us -> 163 us
    reduce_scatter x4, waiting for transfers between devices: 954 us -> 33.6 us  [scatter_blocks(): share = lax.psum_scatter(parts, ('row', 'y'), scatter_dimension=0)]
    all_gather x8 -> x4, waiting for transfers between devices: 481 us -> 88.3 us  [gather_blocks(): found = lax.all_gather(block, ('row', 'y')).reshape(rows, pair, high, wide)]
    unnamed x3 -> x0, blocking collectives: 187 us -> none
    all_gather x0 -> x1, blocking collectives: none -> 58.1 us  [body(): lax.all_gather(jnp.concatenate([first_gain, first_shift, output_bias, sec...]
    reshape x3 -> x22, local copies, waits for them, and re-layouts: 6.84 us -> 57 us  [the longest x4 21.1 us: gather_blocks(): found = lax.all_gather(block, ('row', 'y')).reshape(rows, pair, high, wide)]
    all_to_all x0 -> x3, waiting for transfers between devices: none -> 46.8 us  [the longest x2 46.8 us: images_out(): lax.all_to_all(mine, 'row', split_axis=2, concat_axis=0, tiled=True)]
    psum x6 -> x1, blocking collectives: 89.1 us -> 76.7 us  [body(): lax.psum(jnp.concatenate([wide_sums.reshape(-1), deep_sums.reshape(-1)]),...]
  transfers between devices with their start and end apart: 17 -> 23, of which waited for: 12 -> 10; matrix products, arithmetic and copies ran while one was open for 15% -> 44% of each run, Pallas kernels for 0% -> 0%
where the time goes in v1:
time: 686 us; the launch traced here: 677 us
  waiting for transfers between devices  183 us (27%)
  local copies, waits for them, and re-layouts  163 us (24%)
  blocking collectives  135 us (20%)
  matrix products  117 us (17%)
  other arithmetic  42.8 us (6%)
  starting transfers between devices  20.5 us (3%)
  between operations  15.5 us (2%)
    all_gather x4, waiting for transfers between devices, gather_blocks(): found = lax.all_gather(block, ('row', 'y')).reshape(rows, pair, high, wide)  88.3 us
    psum x1, blocking collectives, body(): lax.psum(jnp.concatenate([wide_sums.reshape(-1), deep_sums.reshape(-1)]),...  76.7 us
    all_gather x1, blocking collectives, body(): lax.all_gather(jnp.concatenate([first_gain, first_shift, output_bias, sec...  58.1 us
    dot_general x28, matrix products, against_rows(): lax.dot_general(left, right, (((1,), (1,)), ((), ())), preferred_element_...  49.2 us
    all_to_all x2, waiting for transfers between devices, images_out(): lax.all_to_all(mine, 'row', split_axis=2, concat_axis=0, tiled=True)  46.8 us
    dot_general x20, matrix products, over_rows(): lax.dot_general(left, right, (((0,), (0,)), ((), ())), preferred_element_...  34.8 us
    reduce_scatter x4, waiting for transfers between devices, scatter_blocks(): share = lax.psum_scatter(parts, ('row', 'y'), scatter_dimension=0)  33.6 us
    dot_general x20, matrix products, product(): return jnp.dot(left, right, preferred_element_type=jnp.float32)  33.3 us
  transfers between devices with their start and end apart: 23, of which 10 were waited for; matrix products, arithmetic and copies ran while one was open for 44% of the time, Pallas kernels for 0%

profile of v1, /device:TPU:0, one launch (start us, length us, event | category | flops | bytes accessed | tf_op | source)
XLA Modules:
  0.0 677.2 jit_solution(8885478903030260996)
XLA Ops:
  9.4 1.8 stack.81
  12.8 2.4 constant_dynamic-slice_fusion.8
  18.5 1.9 copy.131
  20.4 6.2 all-to-all-start
  27.5 58.1 %all-gather = f32[24576]{0:T(1024)S(1)} all-gather(f32[3072]{0:T(1024)S(1)} %constant_dynamic-update-slice_fusion.3), channel_id=2, replica_groups=mesh['dp'=2,'row'=4,'y'=2,'core'=2] {'row','y'}, dimensions={0}, use_global_device_ids=true | all-gather | bytes 110592 | tf_op jit(solution)/shard_map/all_gather | solution.py:183
  87.9 2.0 copy.145
  92.7 2.0 convert_reduce_fusion.2
  96.2 1.8 convert_element_type.120
  97.9 28.6 %all-gather.10.cloned.1.call-done = bf16[2048,768]{1,0:T(8,128)(2,1)} async-done(((bf16[256,768]{1,0:T(8,128)(2,1)}), bf16[2048,768]{1,0:T(8,128)(2,1)}) %all-gather.10.cloned.1.call-update) | async-done | bytes 3145744 | tf_op jit(solution)/shard_map/all_gather | solution.py:78
  126.5 5.1 copy.140
  133.9 3.2 add_convert_fusion
  137.1 16.5 %copy.143 = bf16[577,1536]{0,1:T(8,128)(2,1)} copy(bf16[577,1536]{1,0:T(8,128)(2,1)} %add_convert_fusion) | data formatting | bytes 3545088 | tf_op jit(solution)/shard_map/convert_element_type | solution.py:216
  153.6 4.7 copy.144
  158.3 25.0 %while.22 = (s32[]{:T(128)}, bf16[8,577,64]{1,2,0:T(8,128)(2,1)S(1)}, f32[8,577]{1,0:T(8,128)S(1)}, bf16[8,3,577,64]{3,2,1,0:T(8,128)(2,1)}, s32[]{:T(128)}, /*index=5*/s32[]{:T(128)}, s32[]{}, s32[]{}) while((s32[]{:T(128)}, bf16[8,577,64]{1,2,0:T(8,128)(2,1)S(1)}, f32[8,577]{1,0:T(8,128)S(1)}, bf16[8,3,577,64]{3,2,1,0:T(8,128)(2,1)}, ...), condition=%wide.region_5.6_spmd, body=%wide.region_2.5_spmd.sunk | while | flops 87559744 | bytes 4805289 | solution.py:220
  183.3 3.5 fusion.41
  186.8 2.3 copy.136
  189.2 3.3 reshape.398
  192.4 4.1 copy.153
  196.5 3.9 unstack.12
  200.7 8.5 %copy.146 = bf16[4,2,256,1024]{3,1,2,0:T(2,128)(2,1)} copy(bf16[4,2,256,1024]{3,2,1,0:T(8,128)(2,1)} %bitcast.291) | data formatting | bytes 8388608 | tf_op jit(solution)/shard_map/reshape | solution.py:78
  209.1 5.7 copy.178
  214.9 59.5 %all-gather.16.cloned.1.call-done = bf16[8192,256]{1,0:T(8,128)(2,1)} async-done(((bf16[1024,256]{1,0:T(8,128)(2,1)}), bf16[8192,256]{1,0:T(8,128)(2,1)}) %all-gather.16.cloned.1.call-update) | async-done | bytes 4194320 | tf_op jit(solution)/shard_map/all_gather | solution.py:78
  274.3 5.4 copy.147
  280.8 3.1 fusion.35
  284.4 3.8 multiply_convert_fusion.1
  288.3 4.7 convert_reduce_fusion
  293.0 2.7 fusion.43
  295.8 2.7 fusion.42
  301.9 1.9 collective-permute-done.3
  303.8 2.2 convert_reduce_fusion.3
  306.0 2.0 convolution_convert_fusion.3
  308.0 1.9 reshape.392
  311.2 8.1 %convolution_convert_fusion.2 = bf16[1024,2048]{1,0:T(8,128)(2,1)} fusion(bf16[577,2048]{1,0:T(8,128)(2,1)} %copy-done.28, f32[577,1024]{1,0:T(8,128)} %copy-done.4, f32[1024]{0:T(1024)S(1)} %bitcast.342, f32[1024]{0:T(1024)S(1)} %bitcast.326, f32[577]{0:T(1024)S(1)} %get-tuple-element.179, f32[577]{0:T(1024)S(1)} %get-tuple-element.178), kind=kOutput, calls=%fused_computation.51 | convolution fusion | flops 2425164800 | bytes 8933896 | tf_op jit(solution)/shard_map/dot_general | solution.py:24
  319.4 7.8 %reshape.394 = bf16[4,256,2,1024]{3,2,1,0:T(2,128)(2,1)} reshape(bf16[1024,2048]{1,0:T(8,128)(2,1)} %convolution_convert_fusion.2) | data formatting | bytes 8388608 | tf_op jit(solution)/shard_map/reshape | solution.py:91
  327.2 5.5 copy.165
  332.8 7.5 %convolution_convert_fusion.1 = bf16[2048,1024]{1,0:T(8,128)(2,1)} fusion(bf16[577,2048]{1,0:T(8,128)(2,1)} %copy-done.29, bf16[577,1024]{1,0:T(8,128)(2,1)} %unstack.12), kind=kOutput, calls=%fused_computation.50 | convolution fusion | flops 2422210560 | bytes 7739392 | tf_op jit(solution)/shard_map/dot_general | solution.py:24
  340.3 7.9 %reshape.396 = bf16[2,1024,4,256]{3,2,1,0:T(4,128)(2,1)} reshape(bf16[2048,1024]{1,0:T(8,128)(2,1)} %convolution_convert_fusion.1) | data formatting | bytes 8388608 | tf_op jit(solution)/shard_map/reshape | solution.py:89
  348.2 4.7 copy.166
  357.1 52.8 %while.23 = (s32[]{:T(128)}, bf16[8,3,577,64]{2,3,1,0:T(8,128)(2,1)}, bf16[8,3,577,64]{3,2,1,0:T(8,128)(2,1)}, f32[8,577]{1,0:T(8,128)S(1)}, bf16[8,577,64]{1,2,...) while((s32[]{:T(128)}, bf16[8,3,577,64]{2,3,1,0:T(8,128)(2,1)}, ...), condition=%wide.region_12.13_spmd, body=%wide.region_10.12_spmd.sunk | while | flops 216549824 | bytes 11929535 | solution.py:246
  410.0 6.6 fusion.44
  416.6 4.2 convolution_convert_fusion
  420.8 6.7 reshape.390
  427.5 2.2 copy.163
  431.5 3.7 dynamic-slice_reduce_fusion.2
  437.3 4.8 reduce.20
  442.1 1.9 reshape.430
  444.0 3.6 all-to-all-start.1
  447.7 1.9 convert_reduce_fusion.1
  449.9 26.0 %all-to-all-done.1 = bf16[4,2,36928]{2,1,0:T(2,128)(2,1)S(1)} async-done(((bf16[4,2,36928]{2,1,0:T(2,128)(2,1)}), bf16[4,2,36928]{2,1,0:T(2,128)(2,1)S(1)}, u32[]{:S(2)}, u32[]{:S(2)}) %all-to-all-start.1) | async-done | bytes 590880 | tf_op jit(solution)/shard_map/all_to_all | solution.py:68
  475.9 1.7 reshape.431
  482.1 3.8 multiply_reduce_fusion.2
  485.9 1.9 add_convert_fusion.1
  487.7 3.3 reshape.383
  491.1 3.7 dynamic-slice_reduce_fusion.1
  496.5 4.9 reduce.21
  501.4 1.9 reshape.432
  503.3 3.5 all-to-all-start.2
  508.6 4.3 copy.152
  515.2 20.7 %all-to-all-done.2 = bf16[4,2,36928]{2,1,0:T(2,128)(2,1)S(1)} async-done(((bf16[4,2,36928]{2,1,0:T(2,128)(2,1)}), bf16[4,2,36928]{2,1,0:T(2,128)(2,1)S(1)}, u32[]{:S(2)}, u32[]{:S(2)}) %all-to-all-start.2) | async-done | bytes 590880 | tf_op jit(solution)/shard_map/all_to_all | solution.py:68
  535.9 1.7 reshape.433
  538.8 76.7 %psum.7 = f32[9216]{0:T(1024)S(1)} all-reduce(f32[9216]{0:T(1024)S(1)} %pad_maximum_fusion.3), channel_id=1, replica_groups=mesh['dp'=2,'row'=4,'y'=2,'core'=2] {'dp','row','y'}, use_global_device_ids=true, to_apply=%region_23.24 | all-reduce | flops 9216 | bytes 73728 | tf_op jit(solution)/shard_map/psum | solution.py:280
  619.9 3.7 copy.161
  625.2 33.6 %reduce-scatter.5.cloned.1.call-done = bf16[1,256,768]{2,1,0:T(8,128)(2,1)} async-done(((bf16[8,256,768]{2,1,0:T(8,128)(2,1)}), bf16[1,256,768]{2,1,0:T(8,128)(2,1)}) %reduce-scatter.5.cloned.1.call-update) | async-done | bytes 393232 | tf_op jit(solution)/shard_map/reduce_scatter | solution.py:93
  662.5 6.6 collective-permute-done.8
  (313 shorter events, 130.3 us)
Async XLA Ops:
  7.2 4.0 copy-start.14
  7.2 80.7 %all-gather.12.cloned.1.call-start = ((), (), s32[]{:S(2)}) async-start(), calls=%async_computation.12 | async-start | bytes 1179648 | tf_op jit(solution)/shard_map/all_gather | solution.py:78
  7.9 118.6 %all-gather.10.cloned.1.call-start = ((), (), s32[]{:S(2)}) async-start(), calls=%async_computation.11 | async-start | bytes 3538944 | tf_op jit(solution)/shard_map/all_gather | solution.py:78
  8.7 192.0 %all-gather.14.cloned.1.call-start = ((), (), s32[]{:S(2)}) async-start(), calls=%async_computation.13 | async-start | bytes 4718592 | tf_op jit(solution)/shard_map/all_gather | solution.py:78
  15.8 2.2 collective-permute-start
  18.4 8.9 %copy-start.20 = (f32[256]{0:T(256)S(1)}, f32[256]{0:T(256)}, u32[]{:S(2)}) copy-start(f32[256]{0:T(256)} %param.20) | copy-start | bytes 3076
  18.4 8.9 %copy-start.21 = (f32[256]{0:T(256)S(1)}, f32[256]{0:T(256)}, u32[]{:S(2)}) copy-start(f32[256]{0:T(256)} %param.21) | copy-start | bytes 3076
  18.4 8.9 %copy-start.22 = (f32[256]{0:T(256)S(1)}, f32[256]{0:T(256)}, u32[]{:S(2)}) copy-start(f32[256]{0:T(256)} %param.26) | copy-start | bytes 3076
  18.4 8.9 %copy-start.23 = (f32[256]{0:T(256)S(1)}, f32[256]{0:T(256)}, u32[]{:S(2)}) copy-start(f32[256]{0:T(256)} %param.27) | copy-start | bytes 3076
  18.5 8.9 %copy-start.24 = (f32[256]{0:T(256)S(1)}, f32[256]{0:T(256)}, u32[]{:S(2)}) copy-start(f32[256]{0:T(256)} %param.28) | copy-start | bytes 3076
  18.5 9.0 %copy-start.25 = (f32[256]{0:T(256)S(1)}, f32[256]{0:T(256)}, u32[]{:S(2)}) copy-start(f32[256]{0:T(256)} %param.32) | copy-start | bytes 3076
  18.5 9.0 %copy-start.26 = (f32[256]{0:T(256)S(1)}, f32[256]{0:T(256)}, u32[]{:S(2)}) copy-start(f32[256]{0:T(256)} %param.23) | copy-start | bytes 3076
  18.5 9.0 %copy-start.27 = (f32[256]{0:T(256)S(1)}, f32[256]{0:T(256)}, u32[]{:S(2)}) copy-start(f32[256]{0:T(256)} %param.24) | copy-start | bytes 3076
  18.5 9.0 %copy-start.19 = (f32[1024]{0:T(1024)S(1)}, f32[1024]{0:T(1024)}, u32[]{:S(2)}) copy-start(f32[1024]{0:T(1024)} %param.30) | copy-start | bytes 12292
  20.4 65.2 %all-to-all-start = ((bf16[2,4,577,128]{3,0,2,1:T(2,128)(2,1)}), bf16[2,4,577,128]{3,0,2,1:T(2,128)(2,1)S(1)}, u32[]{:S(2)}, u32[]{:S(2)}) async-start(bf16[2,4,577,128]{3,0,2,1:T(2,128)(2,1)} %copy.131), calls=%async_computation | async-start | bytes 2363392 | tf_op jit(solution)/shard_map/all_to_all | solution.py:55
  26.7 247.7 %all-gather.16.cloned.1.call-start = ((), (), s32[]{:S(2)}) async-start(), calls=%async_computation.14 | async-start | bytes 4718592 | tf_op jit(solution)/shard_map/all_gather | solution.py:78
  27.2 479.8 %reduce-scatter.7.cloned.1.call-start = ((), (), s32[]{:S(2)}) async-start(), calls=%async_computation.8 | async-start | bytes 1179648 | tf_op jit(solution)/shard_map/reduce_scatter | solution.py:93
  87.3 3.8 collective-permute-start.1
  131.6 2.2 copy-start.12
  132.2 1.6 copy-start.9
  186.8 94.0 %collective-permute-start.2 = (f32[577,1024]{1,0:T(8,128)}, f32[577,1024]{1,0:T(8,128)}, u32[]{:S(2)}, u32[]{:S(2)}) collective-permute-start(f32[577,1024]{1,0:T(8,128)} %fusion.41), channel_id=1, source_target_pairs={{0,1},{1,0},{2,3},{3,2},{4,5},{5,4},{6,7},{7,6},{8,9},{9,8},{10,11... | collective-permute-start | bytes 7090184 | tf_op jit(solution)/shard_map/ppermute | solution.py:36
  192.4 88.4 %copy-start = (f32[577,1024]{1,0:T(8,128)}, f32[577,1024]{1,0:T(8,128)S(1)}, u32[]{:S(2)}) copy-start(f32[577,1024]{1,0:T(8,128)S(1)} %reshape.398) | copy-start | bytes 7090180
  280.8 3.6 copy-start.8
  284.0 19.8 %copy-start.4 = (f32[577,1024]{1,0:T(8,128)}, f32[577,1024]{1,0:T(8,128)S(1)}, u32[]{:S(2)}) copy-start(f32[577,1024]{1,0:T(8,128)S(1)} %get-tuple-element.142) | copy-start | bytes 7090180
  284.4 3.8 copy-start.7
  288.2 7.6 %copy-start.29 = (bf16[577,2048]{1,0:T(8,128)(2,1)}, bf16[577,2048]{1,0:T(8,128)(2,1)S(1)}, u32[]{:S(2)}) copy-start(bf16[577,2048]{1,0:T(8,128)(2,1)S(1)} %get-tuple-element.182) | copy-start | bytes 7090180
  293.0 2.7 copy-start.28
  295.7 4.6 collective-permute-start.5
  298.5 5.3 collective-permute-start.3
  306.0 47.2 %copy-start.2 = (f32[577,1024]{1,0:T(8,128)}, f32[577,1024]{1,0:T(8,128)S(1)}, u32[]{:S(2)}) copy-start(f32[577,1024]{1,0:T(8,128)S(1)} %get-tuple-element.139) | copy-start | bytes 7090180
  311.0 306.5 %reduce-scatter.9.cloned.1.call-start = ((), (), s32[]{:S(2)}) async-start(), calls=%async_computation.9 | async-start | bytes 4718592 | tf_op jit(solution)/shard_map/reduce_scatter | solution.py:93
  332.7 285.5 %reduce-scatter.11.cloned.1.call-start = ((), (), s32[]{:S(2)}) async-start(), calls=%async_computation.10 | async-start | bytes 4718592 | tf_op jit(solution)/shard_map/reduce_scatter | solution.py:93
  352.9 1.2 copy-start.5
  352.9 305.8 %reduce-scatter.5.cloned.1.call-start = ((), (), s32[]{:S(2)}) async-start(), calls=%async_computation.7 | async-start | bytes 3538944 | tf_op jit(solution)/shard_map/reduce_scatter | solution.py:93
  409.9 6.6 copy-start.11
  409.9 6.6 copy-start.13
  416.6 65.5 %collective-permute-start.6 = (f32[577,1024]{1,0:T(8,128)}, f32[577,1024]{1,0:T(8,128)}, u32[]{:S(2)}, u32[]{:S(2)}) collective-permute-start(f32[577,1024]{1,0:T(8,128)} %fusion.44), channel_id=1, source_target_pairs={{0,1},{1,0},{2,3},{3,2},{4,5},{5,4},{6,7},{7,6},{8,9},{9,8},{10,11... | collective-permute-start | bytes 7090184 | tf_op jit(solution)/shard_map/ppermute | solution.py:36
  429.7 1.3 copy-start.6
  444.0 31.9 %all-to-all-start.1 = ((bf16[4,2,36928]{2,1,0:T(2,128)(2,1)}), bf16[4,2,36928]{2,1,0:T(2,128)(2,1)S(1)}, u32[]{:S(2)}, u32[]{:S(2)}) async-start(bf16[4,2,36928]{2,1,0:T(2,128)(2,1)} %reshape.430), calls=%async_computation.1 | async-start | bytes 1183744 | tf_op jit(solution)/shard_map/all_to_all | solution.py:68
  477.7 4.4 copy-start.1
  482.0 24.9 %collective-permute-start.4 = (bf16[1154,128]{1,0:T(8,128)(2,1)S(1)}, bf16[1154,128]{1,0:T(8,128)(2,1)S(1)}, u32[]{:S(2)}, u32[]{:S(2)}) collective-permute-start(bf16[1154,128]{1,0:T(8,128)(2,1)S(1)} %dynamic-slice_bitcast_fusion.15), channel_id=1, source_target_pairs={{0,1},{1,0},{2,3},{3,2},{4,5},{5,4},{6,7},{7,6},{8,9},{9,8},{10,11... | collective-permute-start | bytes 886280 | tf_op jit(solution)/shard_map/ppermute | solution.py:36
  482.1 3.8 copy-start.3
  496.5 10.3 %copy-start.10 = (bf16[2,1154,128]{2,1,0:T(8,128)(2,1)S(1)}, bf16[2,1154,128]{2,1,0:T(8,128)(2,1)}, u32[]{:S(2)}) copy-start(bf16[2,1154,128]{2,1,0:T(8,128)(2,1)} %reshape.377) | copy-start | bytes 1772548
  503.3 32.5 %all-to-all-start.2 = ((bf16[4,2,36928]{2,1,0:T(2,128)(2,1)}), bf16[4,2,36928]{2,1,0:T(2,128)(2,1)S(1)}, u32[]{:S(2)}, u32[]{:S(2)}) async-start(bf16[4,2,36928]{2,1,0:T(2,128)(2,1)} %reshape.432), calls=%async_computation.2 | async-start | bytes 1183744 | tf_op jit(solution)/shard_map/all_to_all | solution.py:68
  507.0 7.3 %copy-start.18 = (bf16[1,256,256]{2,1,0:T(8,128)(2,1)S(1)}, bf16[1,256,256]{2,1,0:T(8,128)(2,1)}, u32[]{:S(2)}) copy-start(bf16[1,256,256]{2,1,0:T(8,128)(2,1)} %reduce-scatter.7.cloned.1.call-done) | copy-start | bytes 393220
  507.0 7.3 %collective-permute-start.9 = (bf16[256,256]{1,0:T(8,128)(2,1)}, bf16[256,256]{1,0:T(8,128)(2,1)S(1)}, u32[]{:S(2)}, u32[]{:S(2)}) collective-permute-start(bf16[256,256]{1,0:T(8,128)(2,1)} %bitcast.318), channel_id=1, source_target_pairs={{0,16},{16,0},{1,17},{17,1},{2,18},{18,2},{3,19},{19,3},{4,20},{20... | collective-permute-start | bytes 393224 | tf_op jit(solution)/shard_map/ppermute | solution.py:95
  538.7 79.4 %collective-permute-start.7 = (bf16[1154,128]{1,0:T(8,128)(2,1)S(1)}, bf16[1154,128]{1,0:T(8,128)(2,1)S(1)}, u32[]{:S(2)}, u32[]{:S(2)}) collective-permute-start(bf16[1154,128]{1,0:T(8,128)(2,1)S(1)} %dynamic-slice_bitcast_fusion.14), channel_id=1, source_target_pairs={{0,1},{1,0},{2,3},{3,2},{4,5},{5,4},{6,7},{7,6},{8,9},{9,8},{10,11... | collective-permute-start | bytes 886280 | tf_op jit(solution)/shard_map/ppermute | solution.py:36
  617.5 42.7 %collective-permute-start.10 = (bf16[256,1024]{1,0:T(8,128)(2,1)}, bf16[256,1024]{1,0:T(8,128)(2,1)S(1)}, u32[]{:S(2)}, u32[]{:S(2)}) collective-permute-start(bf16[256,1024]{1,0:T(8,128)(2,1)} %bitcast.315), channel_id=1, source_target_pairs={{0,16},{16,0},{1,17},{17,1},{2,18},{18,2},{3,19},{19,3},{4,20},{20... | collective-permute-start | bytes 1572872 | tf_op jit(solution)/shard_map/ppermute | solution.py:95
  618.3 43.1 %collective-permute-start.11 = (bf16[1024,256]{1,0:T(8,128)(2,1)}, bf16[1024,256]{1,0:T(8,128)(2,1)S(1)}, u32[]{:S(2)}, u32[]{:S(2)}) collective-permute-start(bf16[1024,256]{1,0:T(8,128)(2,1)} %bitcast.316), channel_id=1, source_target_pairs={{0,16},{16,0},{1,17},{17,1},{2,18},{18,2},{3,19},{19,3},{4,20},{20... | collective-permute-start | bytes 1572872 | tf_op jit(solution)/shard_map/ppermute | solution.py:95
  623.6 36.7 %copy-start.15 = (bf16[1,256,1024]{2,1,0:T(8,128)(2,1)S(1)}, bf16[1,256,1024]{2,1,0:T(8,128)(2,1)}, u32[]{:S(2)}) copy-start(bf16[1,256,1024]{2,1,0:T(8,128)(2,1)} %reduce-scatter.9.cloned.1.call-done) | copy-start | bytes 1572868
  624.1 37.3 %copy-start.16 = (bf16[1,1024,256]{2,1,0:T(8,128)(2,1)S(1)}, bf16[1,1024,256]{2,1,0:T(8,128)(2,1)}, u32[]{:S(2)}) copy-start(bf16[1,1024,256]{2,1,0:T(8,128)(2,1)} %reduce-scatter.11.cloned.1.call-done) | copy-start | bytes 1572868
  658.7 10.4 %copy-start.17 = (bf16[1,256,768]{2,1,0:T(8,128)(2,1)S(1)}, bf16[1,256,768]{2,1,0:T(8,128)(2,1)}, u32[]{:S(2)}) copy-start(bf16[1,256,768]{2,1,0:T(8,128)(2,1)} %reduce-scatter.5.cloned.1.call-done) | copy-start | bytes 1179652
  658.7 10.4 %collective-permute-start.8 = (bf16[256,768]{1,0:T(8,128)(2,1)}, bf16[256,768]{1,0:T(8,128)(2,1)S(1)}, u32[]{:S(2)}, u32[]{:S(2)}) collective-permute-start(bf16[256,768]{1,0:T(8,128)(2,1)} %bitcast.317), channel_id=1, source_target_pairs={{0,16},{16,0},{1,17},{17,1},{2,18},{18,2},{3,19},{19,3},{4,20},{20... | collective-permute-start | bytes 1179656 | tf_op jit(solution)/shard_map/ppermute | solution.py:95
Sparse Core Ops, SparseCore 0:
  10.1 54.2 all-gather.11
  66.6 59.8 all-gather.9
  128.6 72.0 all-gather.13
  202.6 71.6 all-gather.15
  311.1 61.5 reduce-scatter.6
  376.6 99.5 reduce-scatter.8
  479.8 100.1 reduce-scatter.10
  584.0 74.6 reduce-scatter.4

commit v2 on v1

--- a/solution.py
+++ b/solution.py
@@ -72,29 +72,55 @@
     return by_core(kept, other, 1).reshape(-1, 2 * half)
 
 
+def swap_sides(piece):
+    return lax.ppermute(piece, "side", [(0, 1), (1, 0)])
+
+
+def by_side(mine, other, axis):
+    first = lax.axis_index("side") == 0
+    return jnp.stack([jnp.where(first, mine, other), jnp.where(first, other, mine)], axis=axis)
+
+
 def gather_blocks(block, split_columns):
     rows, pair = lax.axis_size("row"), lax.axis_size("y")
     high, wide = block.shape
-    found = lax.all_gather(block, ("row", "y")).reshape(rows, pair, high, wide)
+    half = lax.dynamic_index_in_dim(
+        block.reshape(2, high // 2, wide), lax.axis_index("side"), 0, keepdims=False
+    )
+    found = lax.all_gather(half, ("row", "y"))
+    found = by_side(found, swap_sides(found), 1).reshape(rows, pair, high, wide)
     if split_columns:
         return jnp.transpose(found, (1, 2, 0, 3)).reshape(pair * high, rows * wide)
     return jnp.transpose(found, (0, 2, 1, 3)).reshape(rows * high, pair * wide)
 
 
-def scatter_blocks(grad, split_columns):
+def share_halves(grad, split_columns):
     rows, pair = lax.axis_size("row"), lax.axis_size("y")
+    side = lax.axis_index("side")
     grad = grad.astype(jnp.bfloat16)
     high, wide = grad.shape
     if split_columns:
-        parts = jnp.transpose(grad.reshape(pair, high // pair, rows, wide // rows), (2, 0, 1, 3))
+        parts = grad.reshape(pair, 2, high // pair // 2, rows, wide // rows)
+        order = (2, 0, 1, 3)
+        mine = lax.dynamic_index_in_dim(parts, side, 1, keepdims=False)
+        away = lax.dynamic_index_in_dim(parts, 1 - side, 1, keepdims=False)
     else:
-        parts = jnp.transpose(grad.reshape(rows, high // rows, pair, wide // pair), (0, 2, 1, 3))
-    parts = parts.reshape(rows * pair, *parts.shape[2:])
-    share = lax.psum_scatter(parts, ("row", "y"), scatter_dimension=0)
-    if lax.axis_size("dp") == 2:
-        other = lax.ppermute(share, "dp", [(0, 1), (1, 0)])
-        return share.astype(jnp.float32) + other.astype(jnp.float32)
-    return lax.psum(share, "dp").astype(jnp.float32)
+        parts = grad.reshape(rows, 2, high // rows // 2, pair, wide // pair)
+        order = (0, 2, 1, 3)
+        mine = lax.dynamic_index_in_dim(parts, side, 1, keepdims=False)
+        away = lax.dynamic_index_in_dim(parts, 1 - side, 1, keepdims=False)
+    mine = jnp.transpose(mine, order)
+    away = jnp.transpose(away, order)
+    mine = mine.reshape(rows * pair, *mine.shape[2:])
+    came = swap_sides(away.reshape(mine.shape))
+    return (mine.astype(jnp.float32) + came.astype(jnp.float32)).astype(jnp.bfloat16)
+
+
+def scatter_blocks(half):
+    share = lax.psum_scatter(half, ("row", "y"), scatter_dimension=0)
+    share = lax.psum(share, "far")
+    whole = by_side(share, swap_sides(share), 0)
+    return whole.reshape(-1, whole.shape[-1]).astype(jnp.float32)
 
 
 def norm_forward(values_in, norm_gain, norm_shift):
@@ -179,7 +205,6 @@
     block_heads = query_bias.shape[0] // HEAD_DIM
     heads = pair * block_heads
 
-    joined_all = gather_blocks(joined_weight, False)
     small_all = lax.all_gather(
         jnp.concatenate(
             [
@@ -196,6 +221,8 @@
         ),
         ("row", "y"),
     ).reshape(rows, pair, -1)
+    joined_weight, small_all = lax.optimization_barrier((joined_weight, small_all))
+    joined_all = gather_blocks(joined_weight, False)
     wide = small_all[:, 0, : 6 * width].reshape(rows, 6, width)
     wide = jnp.transpose(wide, (1, 0, 2)).reshape(6, -1)
     gain_one, shift_one, out_bias, gain_two, shift_two, ret_bias = (wide[i] for i in range(6))
@@ -207,7 +234,9 @@
     joined_bias = jnp.stack([q_bias, jnp.zeros_like(q_bias), v_bias], axis=1).reshape(-1)
 
     resid, layer_g = images_in(jnp.stack([activations, layer_grad]))
+    output_weight, joined_all = lax.optimization_barrier((output_weight, joined_all))
     output_all = gather_blocks(output_weight, True)
+    hidden_weight, output_all = lax.optimization_barrier((hidden_weight, output_all))
     hidden_all = gather_blocks(hidden_weight, False)
     return_all = gather_blocks(return_weight, True)
     resid = resid.astype(jnp.float32)
@@ -231,24 +260,31 @@
     layer_output = images_out((hidden_in + mixed).astype(jnp.bfloat16))
 
     grad_out = layer_g.astype(jnp.float32)
-    return_weight_grad = scatter_blocks(over_rows(acted, layer_g), True)
+    return_half = share_halves(over_rows(acted, layer_g), True)
     grad_acted = against_rows(layer_g, return_all)
     grad_pre = (grad_acted * gelu_slope(pre_act)).astype(jnp.bfloat16)
-    hidden_weight_grad = scatter_blocks(over_rows(second_out, grad_pre), False)
+    hidden_half = share_halves(over_rows(second_out, grad_pre), False)
     grad_second = core_sum(against_rows(grad_pre, hidden_all))
+    grad_second, return_half = lax.optimization_barrier((grad_second, return_half))
+    return_weight_grad = scatter_blocks(return_half)
     grad_hidden = grad_out + norm_backward(grad_second, normed_two, inv_two, gain_two)
     grad_branch = grad_hidden.astype(jnp.bfloat16)
-    output_weight_grad = scatter_blocks(over_rows(attended, grad_branch), True)
+    output_half = share_halves(over_rows(attended, grad_branch), True)
     grad_attended = against_rows(grad_branch, output_all).astype(jnp.bfloat16)
     grad_heads = jnp.transpose(
         grad_attended.reshape(chip_images, SEQ, heads, HEAD_DIM), (0, 2, 1, 3)
     ).reshape(-1, SEQ, HEAD_DIM)
+    grad_heads, hidden_half, output_half = lax.optimization_barrier(
+        (grad_heads, hidden_half, output_half)
+    )
+    hidden_weight_grad = scatter_blocks(hidden_half)
+    output_weight_grad = scatter_blocks(output_half)
     grad_blocks = lax.map(attend_backward, (blocks, grad_heads, log_total))
     grad_joined = jnp.transpose(
         grad_blocks.astype(jnp.bfloat16).reshape(chip_images, heads, 3, SEQ, HEAD_DIM),
         (0, 3, 1, 2, 4),
     ).reshape(tokens, -1)
-    joined_weight_grad = scatter_blocks(over_rows(first_out, grad_joined), False)
+    joined_weight_grad = scatter_blocks(share_halves(over_rows(first_out, grad_joined), False))
     grad_first = core_sum(against_rows(grad_joined, joined_all))
     input_grad = images_out(
         (grad_hidden + norm_backward(grad_first, normed_one, inv_one, gain_one)).astype(
@@ -278,7 +314,7 @@
         axis=1,
     )
     sums = lax.psum(
-        jnp.concatenate([wide_sums.reshape(-1), deep_sums.reshape(-1)]), ("dp", "row", "y")
+        jnp.concatenate([wide_sums.reshape(-1), deep_sums.reshape(-1)]), ("far", "side", "row", "y")
     )
     wide_sums = sums[: wide_sums.size].reshape(6, rows, width)
     deep_sums = sums[wide_sums.size :].reshape(pair, -1)
@@ -317,11 +353,11 @@
 def solution(mesh):
     shape = mesh.shape
     mesh = Mesh(
-        mesh.devices.reshape(shape["dp"], shape["row"], shape["col"] // 2, 2),
-        ("dp", "row", "y", "core"),
+        mesh.devices.reshape(shape["dp"] // 2, 2, shape["row"], shape["col"] // 2, 2),
+        ("far", "side", "row", "y", "core"),
     )
     in_specs = (
-        P(("dp", "y", "core"), "row"),
+        P(("far", "side", "y", "core"), "row"),
         P("row"),
         P("row"),
         P("row", ("y", "core")),
@@ -335,11 +371,11 @@
         P(("y", "core")),
         P(("y", "core"), "row"),
         P("row"),
-        P(("dp", "y", "core"), "row"),
+        P(("far", "side", "y", "core"), "row"),
     )
     out_specs = (
-        P(("dp", "y", "core"), "row"),
-        P(("dp", "y", "core"), "row"),
+        P(("far", "side", "y", "core"), "row"),
+        P(("far", "side", "y", "core"), "row"),
         P("row"),
         P("row"),
         P("row", ("y", "core")),

time: 686 us -> 790 us (1.15)
  other arithmetic: 42.8 us -> 81.4 us
  waiting for transfers between devices: 183 us -> 213 us
  local copies, waits for them, and re-layouts: 163 us -> 176 us
  starting transfers between devices: 20.5 us -> 30.7 us
    ppermute x4 -> x12, waiting for transfers between devices: 6.63 us -> 97.2 us  [swap_sides(): return lax.ppermute(piece, 'side', [(0, 1), (1, 0)])]
    all_to_all x1, waiting for transfers between devices: 0.01 us -> 42.8 us  [images_in(): lax.all_to_all(column, 'row', split_axis=1, concat_axis=3, tiled=True)]
    all_gather x4 -> x3, waiting for transfers between devices: 88.3 us -> 49.1 us  [gather_blocks(): found = lax.all_gather(half, ('row', 'y'))]
    all_to_all x2, waiting for transfers between devices: 46.8 us -> 12.5 us  [images_out(): lax.all_to_all(mine, 'row', split_axis=2, concat_axis=0, tiled=True)]
    all_gather x0 -> x1, blocking collectives: none -> 31.7 us  [gather_blocks(): found = lax.all_gather(half, ('row', 'y'))]
    all_gather x1, blocking collectives: 58.1 us -> 32.3 us  [body(): lax.all_gather(jnp.concatenate([first_gain, first_shift, output_bias, sec...]
    convert_element_type x0 -> x12, other arithmetic: none -> 25.2 us  [the longest x4 14.6 us: share_halves(): (mine.astype(jnp.float32) + came.astype(jnp.float32)).astype(jnp.bfloat16)]
    reduce_scatter x4, waiting for transfers between devices: 33.6 us -> 8.79 us  [scatter_blocks(): share = lax.psum_scatter(half, ('row', 'y'), scatter_dimension=0)]
  transfers between devices with their start and end apart: 23 -> 30, of which waited for: 10 -> 17; matrix products, arithmetic and copies ran while one was open for 44% -> 40% of each run, Pallas kernels for 0% -> 0%
where the time goes in v2:
time: 790 us; the launch traced here: 780 us
  waiting for transfers between devices  213 us (27%)
  local copies, waits for them, and re-layouts  176 us (22%)
  blocking collectives  139 us (18%)
  matrix products  123 us (16%)
  other arithmetic  81.4 us (10%)
  starting transfers between devices  30.7 us (4%)
  between operations  15.4 us (2%)
    ppermute x12, waiting for transfers between devices, swap_sides(): return lax.ppermute(piece, 'side', [(0, 1), (1, 0)])  97.2 us
    psum x1, blocking collectives, body(): lax.psum(jnp.concatenate([wide_sums.reshape(-1), deep_sums.reshape(-1)]),...  75.4 us
    dot_general x28, matrix products, against_rows(): lax.dot_general(left, right, (((1,), (1,)), ((), ())), preferred_element_...  49.8 us
    all_gather x3, waiting for transfers between devices, gather_blocks(): found = lax.all_gather(half, ('row', 'y'))  49.1 us
    all_to_all x1, waiting for transfers between devices, images_in(): lax.all_to_all(column, 'row', split_axis=1, concat_axis=3, tiled=True)  42.8 us
    dot_general x20, matrix products, over_rows(): lax.dot_general(left, right, (((0,), (0,)), ((), ())), preferred_element_...  38.2 us
    dot_general x20, matrix products, product(): return jnp.dot(left, right, preferred_element_type=jnp.float32)  35.2 us
    unnamed x106, local copies, waits for them, and re-layouts  34.6 us
  transfers between devices with their start and end apart: 30, of which 17 were waited for; matrix products, arithmetic and copies ran while one was open for 40% of the time, Pallas kernels for 0%

profile of v2, /device:TPU:0, one launch (start us, length us, event | category | flops | bytes accessed | tf_op | source)
XLA Modules:
  0.0 779.9 jit_solution(17807119281199726437)
XLA Ops:
  13.5 32.3 %all-gather = f32[24576]{0:T(1024)S(1)} all-gather(f32[3072]{0:T(1024)S(1)} %constant_dynamic-update-slice_fusion.3), channel_id=2, replica_groups=mesh['far'=1,'side'=2,'row'=4,'y'=2,'core'=2] {'row','y'}, dimensions={0}, use_global_device_ids=true | all-gather | bytes 110592 | tf_op jit(solution)/shard_map/all_gather | solution.py:208
  50.9 2.4 constant_dynamic-slice_fusion.20
  58.4 3.5 all-to-all-start
  63.0 42.8 %all-to-all-done = bf16[2,4,577,128]{3,0,2,1:T(2,128)(2,1)S(1)} async-done(((bf16[2,4,577,128]{3,0,2,1:T(2,128)(2,1)}), bf16[2,4,577,128]{3,0,2,1:T(2,128)(2,1)S(1)}, u32[]{:S(2)}, u32[]{:S(2)}) %all-to-all-start) | async-done | bytes 1181728 | tf_op jit(solution)/shard_map/all_to_all | solution.py:55
  116.5 3.3 reshape.419
  119.9 38.0 %all-gather.9.cloned.1.call-done = bf16[8,512,256]{2,1,0:T(8,128)(2,1)} async-done(((bf16[1,512,256]{2,1,0:T(8,128)(2,1)}), bf16[8,512,256]{2,1,0:T(8,128)(2,1)}) %all-gather.9.cloned.1.call-update) | async-done | bytes 2097168 | tf_op jit(solution)/shard_map/all_gather | solution.py:90
  161.8 3.2 copy.164
  165.9 31.7 %all_gather.25 = bf16[8,128,256]{2,1,0:T(8,128)(2,1)S(1)} all-gather(bf16[1,128,256]{2,1,0:T(8,128)(2,1)S(1)} %constant_dynamic-slice_fusion.17), channel_id=1, replica_groups=mesh['far'=1,'side'=2,'row'=4,'y'=2,'core'=2] {'row','y'}, dimensions={0}, use_global_device_ids=true | all-gather | bytes 589824 | tf_op jit(solution)/shard_map/all_gather | solution.py:90
  198.2 3.5 add_convert_fusion
  201.7 2.7 copy.167
  204.5 3.1 copy.168
  207.5 8.1 %collective-permute-done.3 = bf16[8,128,256]{2,1,0:T(8,128)(2,1)S(1)} collective-permute-done((bf16[8,128,256]{2,1,0:T(8,128)(2,1)S(1)}, bf16[8,128,256]{2,1,0:T(8,128)(2,1)S(1)}, u32[]{:S(2)}, u32[]{:S(2)}) %collective-permute-start.3) | collective-permute-done | bytes 524320 | tf_op jit(solution)/shard_map/ppermute | solution.py:76
  218.7 35.0 %while.22 = (s32[]{:T(128)}, bf16[8,577,64]{1,2,0:T(8,128)(2,1)S(1)}, f32[8,577]{1,0:T(8,128)}, bf16[8,3,577,64]{3,2,1,0:T(8,128)(2,1)}, s32[]{:T(128)}, /*index=5*/s32[]{:T(128)}, s32[]{}, s32[]{}) while((s32[]{:T(128)}, bf16[8,577,64]{1,2,0:T(8,128)(2,1)S(1)}, f32[8,577]{1,0:T(8,128)}, bf16[8,3,577,64]{3,2,1,0:T(8,128)(2,1)}, s32[]{:T(128)}, ...), condition=%wide.region_5.6_spmd, body=%wide.region_2.5_spmd.sunk | while | flops 87559744 | bytes 4805289 | solution.py:249
  256.8 10.9 %all-gather.7.cloned.1.call-done = bf16[8,128,1024]{2,1,0:T(8,128)(2,1)} async-done(((bf16[1,128,1024]{2,1,0:T(8,128)(2,1)}), bf16[8,128,1024]{2,1,0:T(8,128)(2,1)}) %all-gather.7.cloned.1.call-update) | async-done | bytes 2097168 | tf_op jit(solution)/shard_map/all_gather | solution.py:90
  269.2 3.2 copy.180
  272.4 4.1 unstack.12
  276.5 2.5 select_bitcast_fusion.1
  279.4 3.2 copy.174
  282.7 3.1 copy.226
  285.9 2.6 fusion.47
  288.5 25.8 %collective-permute-done.5 = bf16[8,128,1024]{2,1,0:T(8,128)(2,1)} collective-permute-done((bf16[8,128,1024]{2,1,0:T(8,128)(2,1)}, bf16[8,128,1024]{2,1,0:T(8,128)(2,1)}, u32[]{:S(2)}, u32[]{:S(2)}) %collective-permute-start.5) | collective-permute-done | bytes 2097184 | tf_op jit(solution)/shard_map/ppermute | solution.py:76
  318.8 8.5 %copy.172 = bf16[4,256,2,1024]{3,2,1,0:T(2,128)(2,1)} copy(bf16[4,256,2,1024]{3,1,2,0:T(8,128)(2,1)} %bitcast.394) | data formatting | bytes 8388608 | tf_op jit(solution)/shard_map/transpose | solution.py:94
  327.3 3.8 copy.224
  331.2 5.3 multiply_convert_fusion.1
  337.9 5.0 convolution_convert_fusion.2
  342.9 7.9 %reshape.400 = bf16[2,2,512,4,256]{4,3,2,1,0:T(4,128)(2,1)} reshape(bf16[2048,1024]{1,0:T(8,128)(2,1)} %convolution_convert_fusion.2) | data formatting | bytes 8388608 | tf_op jit(solution)/shard_map/reshape | solution.py:103
  350.8 5.2 constant_dynamic-slice_fusion.13
  359.1 4.9 convert_reduce_fusion
  365.4 5.4 convolution_convert_fusion.1
  370.8 8.3 %reshape.404 = bf16[4,2,128,2,1024]{4,3,2,1,0:T(2,128)(2,1)} reshape(bf16[1024,2048]{1,0:T(8,128)(2,1)} %convolution_convert_fusion.1) | data formatting | bytes 8388608 | tf_op jit(solution)/shard_map/reshape | solution.py:108
  379.1 5.3 constant_dynamic-slice_fusion.11
  387.3 4.1 fusion.55
  391.4 4.0 fusion.54
  396.3 2.7 fusion.28
  399.0 7.5 collective-permute-done.10
  406.5 3.7 fusion.26
  410.2 38.0 %collective-permute-done.11 = bf16[8,128,1024]{2,1,0:T(8,128)(2,1)} collective-permute-done((bf16[8,128,1024]{2,1,0:T(8,128)(2,1)}, bf16[8,128,1024]{2,1,0:T(8,128)(2,1)}, u32[]{:S(2)}, u32[]{:S(2)}) %collective-permute-start.11) | collective-permute-done | bytes 2097184 | tf_op jit(solution)/shard_map/ppermute | solution.py:76
  448.2 5.0 fusion.25
  453.2 2.9 add.239
  457.4 4.8 convert_reduce_fusion.3
  464.2 2.6 reshape.406
  472.8 7.5 collective-permute-done.12
  486.4 66.1 %while.23 = (s32[]{:T(128)}, bf16[8,3,577,64]{2,3,1,0:T(8,128)(2,1)}, bf16[8,3,577,64]{3,2,1,0:T(8,128)(2,1)}, f32[8,577]{1,0:T(8,128)}, bf16[8,577,64]{1,2,0:T(...) while((s32[]{:T(128)}, bf16[8,3,577,64]{2,3,1,0:T(8,128)(2,1)}, bf16[8,3,577,64]{3,2,1,0:T(8,128)(2,1)}, ...), condition=%wide.region_12.13_spmd, body=%wide.region_10.12_spmd.sunk | while | flops 216549824 | bytes 11602887 | solution.py:282
  552.5 6.3 fusion.56
  558.8 3.7 dynamic-slice_reduce_fusion.2
  564.8 4.8 reduce.20
  571.6 6.8 all-to-all-start.1
  580.5 5.7 convolution_convert_fusion
  586.2 7.5 reshape.417
  593.7 5.2 constant_dynamic-slice_fusion.6
  604.7 3.5 fusion.30
  609.7 3.8 multiply_reduce_fusion.2
  615.3 3.5 reshape.410
  618.8 3.7 dynamic-slice_reduce_fusion.1
  624.1 4.8 reduce.21
  630.8 5.1 all-to-all-start.2
  637.8 3.9 fusion.27
  641.9 4.5 copy.179
  648.7 12.5 %all-to-all-done.2 = bf16[4,2,36928]{2,1,0:T(2,128)(2,1)S(1)} async-done(((bf16[4,2,36928]{2,1,0:T(2,128)(2,1)}), bf16[4,2,36928]{2,1,0:T(2,128)(2,1)S(1)}, u32[]{:S(2)}, u32[]{:S(2)}) %all-to-all-start.2) | async-done | bytes 590880 | tf_op jit(solution)/shard_map/all_to_all | solution.py:68
  664.1 75.4 %psum.6 = f32[9216]{0:T(1024)S(1)} all-reduce(f32[9216]{0:T(1024)S(1)} %pad_maximum_fusion.11), channel_id=1, replica_groups=mesh['far'=1,'side'=2,'row'=4,'y'=2,'core'=2] {'far','side','row','y'}, use_global_device_ids=true, to_apply=%region_23.24 | all-reduce | flops 9216 | bytes 73728 | tf_op jit(solution)/shard_map/psum | solution.py:316
  742.6 3.7 copy.196
  750.4 4.7 collective-permute-done.18
  756.2 8.7 %reduce-scatter.5.cloned.1.call-done = bf16[1,128,768]{2,1,0:T(8,128)(2,1)} async-done(((bf16[8,128,768]{2,1,0:T(8,128)(2,1)}), bf16[1,128,768]{2,1,0:T(8,128)(2,1)}) %reduce-scatter.5.cloned.1.call-update) | async-done | bytes 196624 | tf_op jit(solution)/shard_map/reduce_scatter | solution.py:120
  767.5 3.3 collective-permute-done.16
  (378 shorter events, 210.0 us)
Async XLA Ops:
  7.2 54.8 %copy-start = (bf16[1024,256]{1,0:T(8,128)(2,1)S(1)}, bf16[1024,256]{1,0:T(8,128)(2,1)}, u32[]{:S(2)}) copy-start(bf16[1024,256]{1,0:T(8,128)(2,1)} %param.31) | copy-start | bytes 1572868
  7.2 42.2 %copy-start.29 = (bf16[1154,256]{1,0:T(8,128)(2,1)S(1)}, bf16[1154,256]{1,0:T(8,128)(2,1)}, u32[]{:S(2)}) copy-start(bf16[1154,256]{1,0:T(8,128)(2,1)} %param.33) | copy-start | bytes 1772548
  7.2 99.8 %all-gather.5.cloned.1.call-start = ((), (), s32[]{:S(2)}) async-start(), calls=%async_computation.7 | async-start | bytes 1769472 | tf_op jit(solution)/shard_map/all_gather | solution.py:90
  54.0 2.1 collective-permute-start
  58.4 47.5 %all-to-all-start = ((bf16[2,4,577,128]{3,0,2,1:T(2,128)(2,1)}), bf16[2,4,577,128]{3,0,2,1:T(2,128)(2,1)S(1)}, u32[]{:S(2)}, u32[]{:S(2)}) async-start(bf16[2,4,577,128]{3,0,2,1:T(2,128)(2,1)} %copy.157), calls=%async_computation | async-start | bytes 2363392 | tf_op jit(solution)/shard_map/all_to_all | solution.py:55
  61.9 96.0 %all-gather.9.cloned.1.call-start = ((), (), s32[]{:S(2)}) async-start(), calls=%async_computation.9 | async-start | bytes 2359296 | tf_op jit(solution)/shard_map/all_gather | solution.py:90
  62.8 205.0 %all-gather.7.cloned.1.call-start = ((), (), s32[]{:S(2)}) async-start(), calls=%async_computation.8 | async-start | bytes 2359296 | tf_op jit(solution)/shard_map/all_gather | solution.py:90
  106.5 3.0 collective-permute-start.1
  107.0 52.4 %collective-permute-start.2 = (bf16[8,128,768]{2,1,0:T(8,128)(2,1)}, bf16[8,128,768]{2,1,0:T(8,128)(2,1)}, u32[]{:S(2)}, u32[]{:S(2)}) collective-permute-start(bf16[8,128,768]{2,1,0:T(8,128)(2,1)} %all-gather.5.cloned.1.call-done), channel_id=1, source_target_pairs={{0,16},{16,0},{1,17},{17,1},{2,18},{18,2},{3,19},{19,3},{4,20},{20... | collective-permute-start | bytes 4718600 | tf_op jit(solution)/shard_map/ppermute | solution.py:76
  119.9 78.3 %copy-start.2 = (f32[577,1024]{1,0:T(8,128)}, f32[577,1024]{1,0:T(8,128)S(1)}, u32[]{:S(2)}) copy-start(f32[577,1024]{1,0:T(8,128)S(1)} %reshape.419) | copy-start | bytes 7090180
  157.9 118.6 %collective-permute-start.6 = (bf16[8,512,256]{2,1,0:T(8,128)(2,1)}, bf16[8,512,256]{2,1,0:T(8,128)(2,1)}, u32[]{:S(2)}, u32[]{:S(2)}) collective-permute-start(bf16[8,512,256]{2,1,0:T(8,128)(2,1)} %all-gather.9.cloned.1.call-done), channel_id=1, source_target_pairs={{0,16},{16,0},{1,17},{17,1},{2,18},{18,2},{3,19},{19,3},{4,20},{20... | collective-permute-start | bytes 6291464 | tf_op jit(solution)/shard_map/ppermute | solution.py:76
  165.6 32.6 %copy-start.25 = (bf16[128,8,2,768]{3,1,2,0:T(8,128)(2,1)}, bf16[128,8,2,768]{3,1,2,0:T(8,128)(2,1)S(1)}, u32[]{:S(2)}) copy-start(bf16[128,8,2,768]{3,1,2,0:T(8,128)(2,1)S(1)} %copy.222) | copy-start | bytes 9437188
  197.7 18.0 %collective-permute-start.3 = (bf16[8,128,256]{2,1,0:T(8,128)(2,1)S(1)}, bf16[8,128,256]{2,1,0:T(8,128)(2,1)S(1)}, u32[]{:S(2)}, u32[]{:S(2)}) collective-permute-start(bf16[8,128,256]{2,1,0:T(8,128)(2,1)S(1)} %all_gather.25), channel_id=1, source_target_pairs={{0,16},{16,0},{1,17},{17,1},{2,18},{18,2},{3,19},{19,3},{4,20},{20... | collective-permute-start | bytes 1572872 | tf_op jit(solution)/shard_map/ppermute | solution.py:76
  215.8 2.0 copy-start.31
  215.8 2.8 copy-start.18
  218.6 390.5 %reduce-scatter.7.cloned.1.call-start = ((), (), s32[]{:S(2)}) async-start(), calls=%async_computation.11 | async-start | bytes 589824 | tf_op jit(solution)/shard_map/reduce_scatter | solution.py:120
  256.7 19.7 %copy-start.8 = (f32[577,1024]{1,0:T(8,128)}, f32[577,1024]{1,0:T(8,128)S(1)}, u32[]{:S(2)}) copy-start(f32[577,1024]{1,0:T(8,128)S(1)} %fusion.53) | copy-start | bytes 7090180
  256.8 29.0 %collective-permute-start.4 = (f32[577,1024]{1,0:T(8,128)S(1)}, f32[577,1024]{1,0:T(8,128)}, u32[]{:S(2)}, u32[]{:S(2)}) collective-permute-start(f32[577,1024]{1,0:T(8,128)S(1)} %fusion.53), channel_id=1, source_target_pairs={{0,1},{1,0},{2,3},{3,2},{4,5},{5,4},{6,7},{7,6},{8,9},{9,8},{10,11... | collective-permute-start | bytes 7090184 | tf_op jit(solution)/shard_map/ppermute | solution.py:36
  267.7 46.6 %collective-permute-start.5 = (bf16[8,128,1024]{2,1,0:T(8,128)(2,1)}, bf16[8,128,1024]{2,1,0:T(8,128)(2,1)}, u32[]{:S(2)}, u32[]{:S(2)}) collective-permute-start(bf16[8,128,1024]{2,1,0:T(8,128)(2,1)} %all-gather.7.cloned.1.call-done), channel_id=1, source_target_pairs={{0,16},{16,0},{1,17},{17,1},{2,18},{18,2},{3,19},{19,3},{4,20},{20... | collective-permute-start | bytes 6291464 | tf_op jit(solution)/shard_map/ppermute | solution.py:76
  282.6 3.1 copy-start.3
  282.7 3.3 copy-start.9
  285.9 28.4 %copy-start.26 = (bf16[8,128,1024]{2,1,0:T(8,128)(2,1)S(1)}, bf16[8,128,1024]{2,1,0:T(8,128)(2,1)}, u32[]{:S(2)}) copy-start(bf16[8,128,1024]{2,1,0:T(8,128)(2,1)} %all-gather.7.cloned.1.call-done) | copy-start | bytes 6291460
  288.5 167.6 %copy-start.7 = (f32[577,1024]{1,0:T(8,128)}, f32[577,1024]{1,0:T(8,128)S(1)}, u32[]{:S(2)}) copy-start(f32[577,1024]{1,0:T(8,128)S(1)} %get-tuple-element.163) | copy-start | bytes 7090180
  331.2 5.3 copy-start.23
  331.2 6.7 copy-start.14
  350.8 8.3 %copy-start.21 = (bf16[256,8,4,256]{3,1,2,0:T(8,128)(2,1)S(1)}, bf16[256,8,4,256]{3,1,2,0:T(8,128)(2,1)}, u32[]{:S(2)}) copy-start(bf16[256,8,4,256]{3,1,2,0:T(8,128)(2,1)} %copy.226) | copy-start | bytes 12582916
  350.8 8.3 %copy-start.34 = (f32[577,2048]{1,0:T(8,128)S(1)}, f32[577,2048]{1,0:T(8,128)}, u32[]{:S(2)}) copy-start(f32[577,2048]{1,0:T(8,128)} %get-tuple-element.228) | copy-start | bytes 14180356
  356.0 3.1 copy-start.15
  357.6 48.9 %collective-permute-start.10 = (bf16[8,512,256]{2,1,0:T(8,128)(2,1)}, bf16[8,512,256]{2,1,0:T(8,128)(2,1)}, u32[]{:S(2)}, u32[]{:S(2)}) collective-permute-start(bf16[8,512,256]{2,1,0:T(8,128)(2,1)} %bitcast.73), channel_id=1, source_target_pairs={{0,16},{16,0},{1,17},{17,1},{2,18},{18,2},{3,19},{19,3},{4,20},{20... | collective-permute-start | bytes 6291464 | tf_op jit(solution)/shard_map/ppermute | solution.py:76
  364.0 1.4 copy-start.35
  379.1 7.8 copy-start.36
  384.4 2.9 copy-start.24
  386.3 5.1 copy-start.22
  386.3 5.1 copy-start.38
  386.3 61.9 %collective-permute-start.11 = (bf16[8,128,1024]{2,1,0:T(8,128)(2,1)}, bf16[8,128,1024]{2,1,0:T(8,128)(2,1)}, u32[]{:S(2)}, u32[]{:S(2)}) collective-permute-start(bf16[8,128,1024]{2,1,0:T(8,128)(2,1)} %bitcast.84), channel_id=1, source_target_pairs={{0,16},{16,0},{1,17},{17,1},{2,18},{18,2},{3,19},{19,3},{4,20},{20... | collective-permute-start | bytes 6291464 | tf_op jit(solution)/shard_map/ppermute | solution.py:76
  391.4 4.5 copy-start.13
  391.4 61.8 %collective-permute-start.9 = (f32[577,1024]{1,0:T(8,128)}, f32[577,1024]{1,0:T(8,128)}, u32[]{:S(2)}, u32[]{:S(2)}) collective-permute-start(f32[577,1024]{1,0:T(8,128)} %fusion.55), channel_id=1, source_target_pairs={{0,1},{1,0},{2,3},{3,2},{4,5},{5,4},{6,7},{7,6},{8,9},{9,8},{10,11... | collective-permute-start | bytes 7090184 | tf_op jit(solution)/shard_map/ppermute | solution.py:36
  395.4 61.9 %collective-permute-start.7 = (f32[577,1024]{1,0:T(8,128)}, f32[577,1024]{1,0:T(8,128)}, u32[]{:S(2)}, u32[]{:S(2)}) collective-permute-start(f32[577,1024]{1,0:T(8,128)} %fusion.54), channel_id=1, source_target_pairs={{0,1},{1,0},{2,3},{3,2},{4,5},{5,4},{6,7},{7,6},{8,9},{9,8},{10,11... | collective-permute-start | bytes 7090184 | tf_op jit(solution)/shard_map/ppermute | solution.py:36
  457.4 4.8 copy-start.20
  462.2 8.6 %copy-start.5 = (f32[577,1024]{1,0:T(8,128)}, f32[577,1024]{1,0:T(8,128)S(1)}, u32[]{:S(2)}) copy-start(f32[577,1024]{1,0:T(8,128)S(1)} %get-tuple-element.161) | copy-start | bytes 7090180
  466.8 4.0 copy-start.12
  469.3 11.0 %collective-permute-start.12 = (bf16[8,128,256]{2,1,0:T(8,128)(2,1)}, bf16[8,128,256]{2,1,0:T(8,128)(2,1)}, u32[]{:S(2)}, u32[]{:S(2)}) collective-permute-start(bf16[8,128,256]{2,1,0:T(8,128)(2,1)} %bitcast.92), channel_id=1, source_target_pairs={{0,16},{16,0},{1,17},{17,1},{2,18},{18,2},{3,19},{19,3},{4,20},{20... | collective-permute-start | bytes 1572872 | tf_op jit(solution)/shard_map/ppermute | solution.py:76
  472.7 9.8 %copy-start.11 = (bf16[1,577,4,2,128]{4,1,2,0,3:T(8,128)(2,1)S(1)}, bf16[1,577,4,2,128]{4,1,2,0,3:T(8,128)(2,1)}, u32[]{:S(2)}) copy-start(bf16[1,577,4,2,128]{4,1,2,0,3:T(8,128)(2,1)} %copy-done.10) | copy-start | bytes 3545092
  482.4 259.2 %reduce-scatter.11.cloned.1.call-start = ((), (), s32[]{:S(2)}) async-start(), calls=%async_computation.13 | async-start | bytes 2359296 | tf_op jit(solution)/shard_map/reduce_scatter | solution.py:120
  483.1 2.7 copy-start.17
  486.4 262.1 %reduce-scatter.9.cloned.1.call-start = ((), (), s32[]{:S(2)}) async-start(), calls=%async_computation.12 | async-start | bytes 2359296 | tf_op jit(solution)/shard_map/reduce_scatter | solution.py:120
  558.8 50.9 %collective-permute-start.13 = (f32[577,1024]{1,0:T(8,128)}, f32[577,1024]{1,0:T(8,128)}, u32[]{:S(2)}, u32[]{:S(2)}) collective-permute-start(f32[577,1024]{1,0:T(8,128)} %fusion.56), channel_id=1, source_target_pairs={{0,1},{1,0},{2,3},{3,2},{4,5},{5,4},{6,7},{7,6},{8,9},{9,8},{10,11... | collective-permute-start | bytes 7090184 | tf_op jit(solution)/shard_map/ppermute | solution.py:36
  569.6 10.9 %copy-start.27 = (bf16[577,1024]{1,0:T(8,128)(2,1)S(1)}, bf16[577,1024]{1,0:T(8,128)(2,1)}, u32[]{:S(2)}) copy-start(bf16[577,1024]{1,0:T(8,128)(2,1)} %convert_element_type.231) | copy-start | bytes 3545092
  571.6 30.2 %all-to-all-start.1 = ((bf16[4,2,36928]{2,1,0:T(2,128)(2,1)}), bf16[4,2,36928]{2,1,0:T(2,128)(2,1)S(1)}, u32[]{:S(2)}, u32[]{:S(2)}) async-start(bf16[4,2,36928]{2,1,0:T(2,128)(2,1)} %reshape.455), calls=%async_computation.1 | async-start | bytes 1183744 | tf_op jit(solution)/shard_map/all_to_all | solution.py:68
  600.3 37.5 %collective-permute-start.15 = (bf16[8,128,768]{2,1,0:T(8,128)(2,1)}, bf16[8,128,768]{2,1,0:T(8,128)(2,1)}, u32[]{:S(2)}, u32[]{:S(2)}) collective-permute-start(bf16[8,128,768]{2,1,0:T(8,128)(2,1)} %bitcast.119), channel_id=1, source_target_pairs={{0,16},{16,0},{1,17},{17,1},{2,18},{18,2},{3,19},{19,3},{4,20},{20... | collective-permute-start | bytes 4718600 | tf_op jit(solution)/shard_map/ppermute | solution.py:76
  604.7 3.6 collective-permute-start.8
  604.7 4.9 copy-start.4
  609.1 4.4 copy-start.6
  609.1 38.7 %collective-permute-start.17 = (bf16[128,256]{1,0:T(8,128)(2,1)}, bf16[128,256]{1,0:T(8,128)(2,1)S(1)}, u32[]{:S(2)}, u32[]{:S(2)}) collective-permute-start(bf16[128,256]{1,0:T(8,128)(2,1)} %bitcast.440), channel_id=1, source_target_pairs={{0,16},{16,0},{1,17},{17,1},{2,18},{18,2},{3,19},{19,3},{4,20},{20... | collective-permute-start | bytes 196616 | tf_op jit(solution)/shard_map/ppermute | solution.py:76
  630.8 30.4 %all-to-all-start.2 = ((bf16[4,2,36928]{2,1,0:T(2,128)(2,1)}), bf16[4,2,36928]{2,1,0:T(2,128)(2,1)S(1)}, u32[]{:S(2)}, u32[]{:S(2)}) async-start(bf16[4,2,36928]{2,1,0:T(2,128)(2,1)} %reshape.457), calls=%async_computation.2 | async-start | bytes 1183744 | tf_op jit(solution)/shard_map/all_to_all | solution.py:68
  635.9 5.9 copy-start.28
  635.9 129.0 %reduce-scatter.5.cloned.1.call-start = ((), (), s32[]{:S(2)}) async-start(), calls=%async_computation.10 | async-start | bytes 1769472 | tf_op jit(solution)/shard_map/reduce_scatter | solution.py:120
  641.8 6.0 copy-start.32
  664.0 77.5 %collective-permute-start.14 = (bf16[1154,128]{1,0:T(8,128)(2,1)S(1)}, bf16[1154,128]{1,0:T(8,128)(2,1)S(1)}, u32[]{:S(2)}, u32[]{:S(2)}) collective-permute-start(bf16[1154,128]{1,0:T(8,128)(2,1)S(1)} %dynamic-slice_bitcast_fusion.14), channel_id=1, source_target_pairs={{0,1},{1,0},{2,3},{3,2},{4,5},{5,4},{6,7},{7,6},{8,9},{9,8},{10,11... | collective-permute-start | bytes 886280 | tf_op jit(solution)/shard_map/ppermute | solution.py:36
  741.7 6.6 collective-permute-start.19
  746.3 2.0 copy-start.30
  748.4 6.6 collective-permute-start.18
  756.1 16.7 %copy-start.1 = (bf16[1024,256]{1,0:T(8,128)(2,1)S(1)}, bf16[1024,256]{1,0:T(8,128)(2,1)}, u32[]{:S(2)}) copy-start(bf16[1024,256]{1,0:T(8,128)(2,1)} %param.31) | copy-start | bytes 1572868
  764.9 5.9 collective-permute-start.16
  (5 other events, 5.4 us)
Sparse Core Ops, SparseCore 0:
  47.7 59.2 all-gather.4
  109.7 48.1 all-gather.8
  218.7 48.9 all-gather.6
  482.5 63.5 reduce-scatter.6
  550.0 66.8 reduce-scatter.10
  620.7 76.3 reduce-scatter.8
  700.9 63.9 reduce-scatter.4
